TPU v7x, 32 devices: a whole 2x2x4 slice. The times are simulated.
32 devices in a mesh: tm: 4 (over y, core), space: 8 (over z, x).
Axes of the slice: x: 2, y: 2, z: 4, core: 2. Of those that a mesh axis runs over, the one named last changes fastest.
Arguments:
- rhs_state: float32 [4, 4, 128, 1280], P('tm', None, 'space'), may hold values from -12 to 12
- rhs_obs: float32 [4, 4, 4, 128, 1280], P('tm', None, None, 'space'), may hold values from -12 to 12
- wind_east: float32 [4, 4, 4, 128, 1280], P('tm', None, None, 'space'), may hold values from -0.45 to 0.45
- wind_north: float32 [4, 4, 4, 128, 1280], P('tm', None, None, 'space'), may hold values from -0.45 to 0.45
- model_var: float32 [4, 4, 128, 1280], P('tm', None, 'space'), may hold values from 0.5 to 2
- obs_var: float32 [4, 4, 4, 128, 1280], P('tm', None, None, 'space'), may hold values from 0.5 to 2
- obs_mask: int32 [4, 4, 4, 128, 1280], P('tm', None, None, 'space'), may hold values 0 or 1
Outputs:
- dual_model: float32 [4, 4, 128, 1280], P('tm', None, 'space')
- dual_obs: float32 [4, 4, 4, 128, 1280], P('tm', None, None, 'space')
- increment: float32 [4, 4, 128, 1280], P('tm', None, 'space')
All inputs are finite; a program needn't handle non-finite values. No bound on the sum of `obs_mask` on one device may be relied on, other than what follows from the above.
Results may differ from a plain program's by a relative error of at most 0.0001.
Values sent between devices are 32-bit elements; how exact they have to be, the bound alone decides.
A program may use at most 64 MiB of HBM per device.

v0:
```python
import jax
import jax.numpy as jnp
from jax import lax
from jax.sharding import PartitionSpec as P

ITERS = 2


KAPPA = 0.12


def extended(cells, sides, width):
    for axis, dim in sides:
        count = lax.axis_size(axis)
        ends = count - 1
        head = lax.slice_in_dim(cells, 0, width, axis=dim)
        tail = lax.slice_in_dim(cells, cells.shape[dim] - width, cells.shape[dim], axis=dim)
        cells = jnp.concatenate(
            [
                lax.ppermute(tail, axis, [(i, (i + 1) % count) for i in range(ends)]),
                cells,
                lax.ppermute(head, axis, [((i + 1) % count, i) for i in range(ends)]),
            ],
            axis=dim,
        )
    return cells


def passed_along(block, axis, distance):
    devices = range(lax.axis_size(axis))
    route = [(i - distance, i) for i in devices if i - distance in devices]
    return lax.ppermute(block, axis, route)


def forward_step(padded, east_c, north_c):
    cells = padded[..., 1:-1, :]
    upper = padded[..., 2:, :]
    lower = padded[..., :-2, :]
    after = jnp.roll(cells, -1, -1)
    before = jnp.roll(cells, 1, -1)
    return (
        cells
        - 0.5 * east_c * (after - before)
        - 0.5 * north_c * (upper - lower)
        + KAPPA * (after + before + upper + lower - 4.0 * cells)
    )


def adjoint_step(padded, weighted, east_c):
    cells = padded[..., 1:-1, :]
    flux = east_c * cells
    along = jnp.roll(KAPPA * cells - 0.5 * flux, 1, -1) + jnp.roll(
        KAPPA * cells + 0.5 * flux, -1, -1
    )
    across = (
        KAPPA * padded[..., :-2, :]
        - 0.5 * weighted[..., :-2, :]
        + KAPPA * padded[..., 2:, :]
        + 0.5 * weighted[..., 2:, :]
    )
    return (1.0 - 4.0 * KAPPA) * cells + along + across


def on_device(rhs_state, rhs_obs, wind_east, wind_north, model_var, obs_var, obs_mask):
    b_lam = rhs_state[0]
    b_dual = rhs_obs[0]
    east_all = wind_east[0]
    north_all = wind_north[0]
    state_var = model_var[0]
    error_var = obs_var[0]
    mask = obs_mask[0].astype(jnp.float32)
    steps = east_all.shape[0]

    def forward(delta):
        current = delta
        observed = []
        for j in range(steps):
            padded = extended(current, (("space", 1),), 1)
            current = forward_step(padded, east_all[j], north_all[j])
            observed.append(mask[j] * current)
        return (current, jnp.stack(observed, 0))

    def adjoint(start, dual):
        current = start
        for j in reversed(range(steps)):
            current = current + mask[j] * dual[j]
            paired = jnp.stack([current, north_all[j] * current], 0)
            padded = extended(paired, (("space", 2),), 1)
            current = adjoint_step(padded[0], padded[1], east_all[j])
        return current

    def operator(lam, dual, delta):
        final, observed = forward(delta)
        earlier = passed_along(final, "tm", 1)
        later = passed_along(lam, "tm", -1)
        out_lam = state_var * lam + delta - earlier
        out_dual = error_var * dual + observed
        out_delta = lam + adjoint(-later, dual)
        return (out_lam, out_dual, out_delta)

    res = (b_lam, b_dual, jnp.zeros_like(b_lam))
    sol = (jnp.zeros_like(b_lam), jnp.zeros_like(b_dual), jnp.zeros_like(b_lam))
    for step in range(ITERS):
        image = operator(*res)
        inner = sum((jnp.sum(p * q) for p, q in zip(res, image)))
        square = sum((jnp.sum(q * q) for q in image))
        inner, square = lax.psum((inner, square), ("tm", "space"))
        alpha = inner / square
        sol = tuple((s + alpha * p for s, p in zip(sol, res)))
        if step + 1 < ITERS:
            res = tuple((p - alpha * q for p, q in zip(res, image)))
    return (sol[0][None], sol[1][None], sol[2][None])


def solution(mesh):
    return jax.shard_map(
        on_device,
        mesh=mesh,
        in_specs=(
            P("tm", None, "space", None),
            P("tm", None, None, "space", None),
            P("tm", None, None, "space", None),
            P("tm", None, None, "space", None),
            P("tm", None, "space", None),
            P("tm", None, None, "space", None),
            P("tm", None, None, "space", None),
        ),
        out_specs=(
            P("tm", None, "space", None),
            P("tm", None, None, "space", None),
            P("tm", None, "space", None),
        ),
        check_vma=False,
    )
```

profile of v0, /device:TPU:0, one launch (start us, length us, event | category | flops | bytes accessed | tf_op | source)
XLA Modules:
  0.0 274.7 jit_solution(9981716543908390969)
XLA Ops:
  0.6 1.3 collective-permute-start.9
  1.9 1.3 collective-permute-start
  3.2 5.5 %collective-permute-start.1 = (f32[4,1,1280]{2,1,0:T(1,128)S(1)}, f32[4,1,1280]{2,1,0:T(1,128)S(1)}, u32[]{:S(2)}, u32[]{:S(2)}) collective-permute-start(f32[4,1,1280]{2,1,0:T(1,128)S(1)} %broadcast.39), channel_id=1, source_target_pairs={{0,1},{1,2},{2,3},{3,4},{4,5},{5,6},{6,7},{8,9},{9,10},{10,11},{11... | collective-permute-start | bytes 61448 | tf_op jit(solution)/shard_map/ppermute | solution.py:20
  8.8 1.6 convert_element_type.4
  10.5 0.4 copy-done.1
  10.9 1.9 fusion.97
  12.9 4.8 %collective-permute-start.10 = (f32[2,4,1,1280]{3,2,1,0:T(1,128)S(1)}, f32[2,4,1,1280]{3,2,1,0:T(1,128)S(1)}, u32[]{:S(2)}, u32[]{:S(2)}) collective-permute-start(f32[2,4,1,1280]{3,2,1,0:T(1,128)S(1)} %get-tuple-element.113), channel_id=1, source_target_pairs={{0,1},{1,2},{2,3},{3,4},{4,5},{5,6},{6,7},{8,9},{9,10},{10,11},{11... | collective-permute-start | bytes 122888 | tf_op jit(solution)/shard_map/ppermute | solution.py:20
  17.7 1.3 collective-permute-start.11
  19.4 4.9 %collective-permute-done.11 = f32[2,4,1,1280]{3,2,1,0:T(1,128)S(1)} collective-permute-done((f32[2,4,1,1280]{3,2,1,0:T(1,128)S(1)}, f32[2,4,1,1280]{3,2,1,0:T(1,128)S(1)}, u32[]{:S(2)}, u32[]{:S(2)}) %collective-permute-start.11) | collective-permute-done | bytes 40992 | tf_op jit(solution)/shard_map/ppermute | solution.py:22
  24.8 1.0 copy-done.3
  26.1 4.8 %collective-permute-start.12 = (f32[2,4,1,1280]{3,2,1,0:T(1,128)S(1)}, f32[2,4,1,1280]{3,2,1,0:T(1,128)S(1)}, u32[]{:S(2)}, u32[]{:S(2)}) collective-permute-start(f32[2,4,1,1280]{3,2,1,0:T(1,128)S(1)} %get-tuple-element.111), channel_id=1, source_target_pairs={{0,1},{1,2},{2,3},{3,4},{4,5},{5,6},{6,7},{8,9},{9,10},{10,11},{11... | collective-permute-start | bytes 122888 | tf_op jit(solution)/shard_map/ppermute | solution.py:20
  30.9 1.3 collective-permute-start.13
  32.3 1.3 collective-permute-start.2
  33.6 5.2 %collective-permute-start.3 = (f32[4,1,1280]{2,1,0:T(1,128)S(1)}, f32[4,1,1280]{2,1,0:T(1,128)S(1)}, u32[]{:S(2)}, u32[]{:S(2)}) collective-permute-start(f32[4,1,1280]{2,1,0:T(1,128)S(1)} %get-tuple-element.158), channel_id=1, source_target_pairs={{0,1},{1,2},{2,3},{3,4},{4,5},{5,6},{6,7},{8,9},{9,10},{10,11},{11... | collective-permute-start | bytes 61448 | tf_op jit(solution)/shard_map/ppermute | solution.py:20
  39.0 1.2 collective-permute-done.3
  40.3 1.1 fusion.93
  42.1 4.8 %collective-permute-start.14 = (f32[2,4,1,1280]{3,2,1,0:T(1,128)S(1)}, f32[2,4,1,1280]{3,2,1,0:T(1,128)S(1)}, u32[]{:S(2)}, u32[]{:S(2)}) collective-permute-start(f32[2,4,1,1280]{3,2,1,0:T(1,128)S(1)} %get-tuple-element.109), channel_id=1, source_target_pairs={{0,1},{1,2},{2,3},{3,4},{4,5},{5,6},{6,7},{8,9},{9,10},{10,11},{11... | collective-permute-start | bytes 122888 | tf_op jit(solution)/shard_map/ppermute | solution.py:20
  46.9 1.3 collective-permute-start.15
  48.3 1.3 collective-permute-start.4
  49.6 6.4 %collective-permute-start.5 = (f32[4,1,1280]{2,1,0:T(1,128)S(1)}, f32[4,1,1280]{2,1,0:T(1,128)S(1)}, u32[]{:S(2)}, u32[]{:S(2)}) collective-permute-start(f32[4,1,1280]{2,1,0:T(1,128)S(1)} %get-tuple-element.152), channel_id=1, source_target_pairs={{0,1},{1,2},{2,3},{3,4},{4,5},{5,6},{6,7},{8,9},{9,10},{10,11},{11... | collective-permute-start | bytes 61448 | tf_op jit(solution)/shard_map/ppermute | solution.py:20
  56.2 1.2 collective-permute-done.5
  57.4 1.1 fusion.91
  59.3 4.8 %collective-permute-start.16 = (f32[2,4,1,1280]{3,2,1,0:T(1,128)S(1)}, f32[2,4,1,1280]{3,2,1,0:T(1,128)S(1)}, u32[]{:S(2)}, u32[]{:S(2)}) collective-permute-start(f32[2,4,1,1280]{3,2,1,0:T(1,128)S(1)} %get-tuple-element.107), channel_id=1, source_target_pairs={{0,1},{1,2},{2,3},{3,4},{4,5},{5,6},{6,7},{8,9},{9,10},{10,11},{11... | collective-permute-start | bytes 122888 | tf_op jit(solution)/shard_map/ppermute | solution.py:20
  64.1 1.3 collective-permute-start.17
  65.5 1.3 collective-permute-start.6
  66.8 6.4 %collective-permute-start.7 = (f32[4,1,1280]{2,1,0:T(1,128)S(1)}, f32[4,1,1280]{2,1,0:T(1,128)S(1)}, u32[]{:S(2)}, u32[]{:S(2)}) collective-permute-start(f32[4,1,1280]{2,1,0:T(1,128)S(1)} %get-tuple-element.146), channel_id=1, source_target_pairs={{0,1},{1,2},{2,3},{3,4},{4,5},{5,6},{6,7},{8,9},{9,10},{10,11},{11... | collective-permute-start | bytes 61448 | tf_op jit(solution)/shard_map/ppermute | solution.py:20
  73.4 1.2 collective-permute-done.7
  74.6 1.1 fusion.89
  75.7 1.4 collective-permute-start.8
  77.4 2.2 multiply_reduce_fusion.2
  79.6 1.0 multiply_reduce_fusion.7
  84.4 48.4 %all-reduce.4 = (f32[]{:T(128)}, f32[]{:T(128)}) all-reduce(f32[]{:T(128)S(6)} %add.375, f32[]{:T(128)S(6)} %add.377), channel_id=1, replica_groups=mesh['tm'=4,'space'=8] {'tm','space'}, use_global_device_ids=true, to_apply=%region_3.4 | all-reduce | flops 2 | bytes 16 | tf_op jit(solution)/shard_map/psum | solution.py:107
  134.4 1.4 collective-permute-start.18
  135.8 4.8 %collective-permute-start.19 = (f32[4,1,1280]{2,1,0:T(1,128)S(1)}, f32[4,1,1280]{2,1,0:T(1,128)S(1)}, u32[]{:S(2)}, u32[]{:S(2)}) collective-permute-start(f32[4,1,1280]{2,1,0:T(1,128)S(1)} %get-tuple-element.138), channel_id=1, source_target_pairs={{0,1},{1,2},{2,3},{3,4},{4,5},{5,6},{6,7},{8,9},{9,10},{10,11},{11... | collective-permute-start | bytes 61448 | tf_op jit(solution)/shard_map/ppermute | solution.py:20
  140.8 1.3 collective-permute-start.27
  142.7 1.3 collective-permute-start.20
  144.0 5.4 %collective-permute-start.21 = (f32[4,1,1280]{2,1,0:T(1,128)S(1)}, f32[4,1,1280]{2,1,0:T(1,128)S(1)}, u32[]{:S(2)}, u32[]{:S(2)}) collective-permute-start(f32[4,1,1280]{2,1,0:T(1,128)S(1)} %get-tuple-element.132), channel_id=1, source_target_pairs={{0,1},{1,2},{2,3},{3,4},{4,5},{5,6},{6,7},{8,9},{9,10},{10,11},{11... | collective-permute-start | bytes 61448 | tf_op jit(solution)/shard_map/ppermute | solution.py:20
  149.5 1.4 collective-permute-done.21
  151.4 1.3 collective-permute-start.22
  152.7 5.7 %collective-permute-start.23 = (f32[4,1,1280]{2,1,0:T(1,128)S(1)}, f32[4,1,1280]{2,1,0:T(1,128)S(1)}, u32[]{:S(2)}, u32[]{:S(2)}) collective-permute-start(f32[4,1,1280]{2,1,0:T(1,128)S(1)} %get-tuple-element.126), channel_id=1, source_target_pairs={{0,1},{1,2},{2,3},{3,4},{4,5},{5,6},{6,7},{8,9},{9,10},{10,11},{11... | collective-permute-start | bytes 61448 | tf_op jit(solution)/shard_map/ppermute | solution.py:20
  158.5 1.4 collective-permute-done.23
  160.4 1.4 collective-permute-start.24
  161.9 5.7 %collective-permute-start.25 = (f32[4,1,1280]{2,1,0:T(1,128)S(1)}, f32[4,1,1280]{2,1,0:T(1,128)S(1)}, u32[]{:S(2)}, u32[]{:S(2)}) collective-permute-start(f32[4,1,1280]{2,1,0:T(1,128)S(1)} %get-tuple-element.120), channel_id=1, source_target_pairs={{0,1},{1,2},{2,3},{3,4},{4,5},{5,6},{6,7},{8,9},{9,10},{10,11},{11... | collective-permute-start | bytes 61448 | tf_op jit(solution)/shard_map/ppermute | solution.py:20
  167.7 1.4 collective-permute-done.25
  169.4 1.0 copy-done.4
  170.4 0.4 copy-done.7
  170.8 1.4 multiply_reduce_fusion
  172.3 5.1 %collective-permute-start.28 = (f32[2,4,1,1280]{3,2,1,0:T(1,128)S(1)}, f32[2,4,1,1280]{3,2,1,0:T(1,128)S(1)}, u32[]{:S(2)}, u32[]{:S(2)}) collective-permute-start(f32[2,4,1,1280]{3,2,1,0:T(1,128)S(1)} %get-tuple-element.105), channel_id=1, source_target_pairs={{0,1},{1,2},{2,3},{3,4},{4,5},{5,6},{6,7},{8,9},{9,10},{10,11},{11... | collective-permute-start | bytes 122888 | tf_op jit(solution)/shard_map/ppermute | solution.py:20
  177.4 1.5 collective-permute-start.29
  179.1 5.4 %collective-permute-done.29 = f32[2,4,1,1280]{3,2,1,0:T(1,128)S(1)} collective-permute-done((f32[2,4,1,1280]{3,2,1,0:T(1,128)S(1)}, f32[2,4,1,1280]{3,2,1,0:T(1,128)S(1)}, u32[]{:S(2)}, u32[]{:S(2)}) %collective-permute-start.29) | collective-permute-done | bytes 40992 | tf_op jit(solution)/shard_map/ppermute | solution.py:22
  185.4 4.8 %collective-permute-start.30 = (f32[2,4,1,1280]{3,2,1,0:T(1,128)S(1)}, f32[2,4,1,1280]{3,2,1,0:T(1,128)S(1)}, u32[]{:S(2)}, u32[]{:S(2)}) collective-permute-start(f32[2,4,1,1280]{3,2,1,0:T(1,128)S(1)} %get-tuple-element.103), channel_id=1, source_target_pairs={{0,1},{1,2},{2,3},{3,4},{4,5},{5,6},{6,7},{8,9},{9,10},{10,11},{11... | collective-permute-start | bytes 122888 | tf_op jit(solution)/shard_map/ppermute | solution.py:20
  190.3 1.3 collective-permute-start.31
  191.9 4.2 %collective-permute-done.31 = f32[2,4,1,1280]{3,2,1,0:T(1,128)S(1)} collective-permute-done((f32[2,4,1,1280]{3,2,1,0:T(1,128)S(1)}, f32[2,4,1,1280]{3,2,1,0:T(1,128)S(1)}, u32[]{:S(2)}, u32[]{:S(2)}) %collective-permute-start.31) | collective-permute-done | bytes 40992 | tf_op jit(solution)/shard_map/ppermute | solution.py:22
  197.1 4.0 %collective-permute-start.32 = (f32[2,4,1,1280]{3,2,1,0:T(1,128)S(1)}, f32[2,4,1,1280]{3,2,1,0:T(1,128)S(1)}, u32[]{:S(2)}, u32[]{:S(2)}) collective-permute-start(f32[2,4,1,1280]{3,2,1,0:T(1,128)S(1)} %get-tuple-element.101), channel_id=1, source_target_pairs={{0,1},{1,2},{2,3},{3,4},{4,5},{5,6},{6,7},{8,9},{9,10},{10,11},{11... | collective-permute-start | bytes 122888 | tf_op jit(solution)/shard_map/ppermute | solution.py:20
  201.0 1.3 collective-permute-start.33
  202.7 4.2 %collective-permute-done.33 = f32[2,4,1,1280]{3,2,1,0:T(1,128)S(1)} collective-permute-done((f32[2,4,1,1280]{3,2,1,0:T(1,128)S(1)}, f32[2,4,1,1280]{3,2,1,0:T(1,128)S(1)}, u32[]{:S(2)}, u32[]{:S(2)}) %collective-permute-start.33) | collective-permute-done | bytes 40992 | tf_op jit(solution)/shard_map/ppermute | solution.py:22
  207.8 4.8 %collective-permute-start.34 = (f32[2,4,1,1280]{3,2,1,0:T(1,128)S(1)}, f32[2,4,1,1280]{3,2,1,0:T(1,128)S(1)}, u32[]{:S(2)}, u32[]{:S(2)}) collective-permute-start(f32[2,4,1,1280]{3,2,1,0:T(1,128)S(1)} %get-tuple-element.99), channel_id=1, source_target_pairs={{0,1},{1,2},{2,3},{3,4},{4,5},{5,6},{6,7},{8,9},{9,10},{10,11},{11... | collective-permute-start | bytes 122888 | tf_op jit(solution)/shard_map/ppermute | solution.py:20
  212.6 1.3 collective-permute-start.35
  213.9 1.3 collective-permute-start.26
  215.3 3.3 %collective-permute-done.35 = f32[2,4,1,1280]{3,2,1,0:T(1,128)S(1)} collective-permute-done((f32[2,4,1,1280]{3,2,1,0:T(1,128)S(1)}, f32[2,4,1,1280]{3,2,1,0:T(1,128)S(1)}, u32[]{:S(2)}, u32[]{:S(2)}) %collective-permute-start.35) | collective-permute-done | bytes 40992 | tf_op jit(solution)/shard_map/ppermute | solution.py:22
  219.1 1.1 multiply_reduce_fusion.3
  224.1 44.7 %all-reduce.3 = (f32[]{:T(128)}, f32[]{:T(128)}) all-reduce(f32[]{:T(128)S(6)} %add.426, f32[]{:T(128)S(6)} %add.428), channel_id=1, replica_groups=mesh['tm'=4,'space'=8] {'tm','space'}, use_global_device_ids=true, to_apply=%region_11.12 | all-reduce | flops 2 | bytes 16 | tf_op jit(solution)/shard_map/psum | solution.py:107
  270.2 2.0 add_bitcast_fusion
  272.2 2.6 fusion.3
  (146 shorter events, 10.7 us)
Async XLA Ops:
  0.6 9.8 %collective-permute-start.9 = (f32[4,16,1280]{2,1,0:T(8,128)}, f32[4,16,1280]{2,1,0:T(8,128)S(1)}, u32[]{:S(2)}, u32[]{:S(2)}) collective-permute-start(f32[4,16,1280]{2,1,0:T(8,128)} %bitcast.425), channel_id=1, source_target_pairs={{8,0},{16,8},{24,16},{9,1},{17,9},{25,17},{10,2},{18,10},{26,18},{... | collective-permute-start | bytes 983048 | tf_op jit(solution)/shard_map/ppermute | solution.py:32
  1.9 8.4 %collective-permute-start = (f32[4,1,1280]{2,1,0:T(1,128)S(1)}, f32[4,1,1280]{2,1,0:T(1,128)S(1)}, u32[]{:S(2)}, u32[]{:S(2)}) collective-permute-start(f32[4,1,1280]{2,1,0:T(1,128)S(1)} %broadcast.39), channel_id=1, source_target_pairs={{1,0},{2,1},{3,2},{4,3},{5,4},{6,5},{7,6},{9,8},{10,9},{11,10},{12... | collective-permute-start | bytes 61448 | tf_op jit(solution)/shard_map/ppermute | solution.py:22
  3.2 7.1 %collective-permute-start.1 = (f32[4,1,1280]{2,1,0:T(1,128)S(1)}, f32[4,1,1280]{2,1,0:T(1,128)S(1)}, u32[]{:S(2)}, u32[]{:S(2)}) collective-permute-start(f32[4,1,1280]{2,1,0:T(1,128)S(1)} %broadcast.39), channel_id=1, source_target_pairs={{0,1},{1,2},{2,3},{3,4},{4,5},{5,6},{6,7},{8,9},{9,10},{10,11},{11... | collective-permute-start | bytes 61448 | tf_op jit(solution)/shard_map/ppermute | solution.py:20
  8.8 1.7 copy-start
  8.8 2.1 copy-start.1
  12.9 6.5 %collective-permute-start.10 = (f32[2,4,1,1280]{3,2,1,0:T(1,128)S(1)}, f32[2,4,1,1280]{3,2,1,0:T(1,128)S(1)}, u32[]{:S(2)}, u32[]{:S(2)}) collective-permute-start(f32[2,4,1,1280]{3,2,1,0:T(1,128)S(1)} %get-tuple-element.113), channel_id=1, source_target_pairs={{0,1},{1,2},{2,3},{3,4},{4,5},{5,6},{6,7},{8,9},{9,10},{10,11},{11... | collective-permute-start | bytes 122888 | tf_op jit(solution)/shard_map/ppermute | solution.py:20
  17.7 6.5 %collective-permute-start.11 = (f32[2,4,1,1280]{3,2,1,0:T(1,128)S(1)}, f32[2,4,1,1280]{3,2,1,0:T(1,128)S(1)}, u32[]{:S(2)}, u32[]{:S(2)}) collective-permute-start(f32[2,4,1,1280]{3,2,1,0:T(1,128)S(1)} %get-tuple-element.114), channel_id=1, source_target_pairs={{1,0},{2,1},{3,2},{4,3},{5,4},{6,5},{7,6},{9,8},{10,9},{11,10},{12... | collective-permute-start | bytes 122888 | tf_op jit(solution)/shard_map/ppermute | solution.py:22
  24.4 1.3 copy-start.3
  26.1 12.7 %collective-permute-start.12 = (f32[2,4,1,1280]{3,2,1,0:T(1,128)S(1)}, f32[2,4,1,1280]{3,2,1,0:T(1,128)S(1)}, u32[]{:S(2)}, u32[]{:S(2)}) collective-permute-start(f32[2,4,1,1280]{3,2,1,0:T(1,128)S(1)} %get-tuple-element.111), channel_id=1, source_target_pairs={{0,1},{1,2},{2,3},{3,4},{4,5},{5,6},{6,7},{8,9},{9,10},{10,11},{11... | collective-permute-start | bytes 122888 | tf_op jit(solution)/shard_map/ppermute | solution.py:20
  30.9 7.9 %collective-permute-start.13 = (f32[2,4,1,1280]{3,2,1,0:T(1,128)S(1)}, f32[2,4,1,1280]{3,2,1,0:T(1,128)S(1)}, u32[]{:S(2)}, u32[]{:S(2)}) collective-permute-start(f32[2,4,1,1280]{3,2,1,0:T(1,128)S(1)} %get-tuple-element.112), channel_id=1, source_target_pairs={{1,0},{2,1},{3,2},{4,3},{5,4},{6,5},{7,6},{9,8},{10,9},{11,10},{12... | collective-permute-start | bytes 122888 | tf_op jit(solution)/shard_map/ppermute | solution.py:22
  32.3 6.7 %collective-permute-start.2 = (f32[4,1,1280]{2,1,0:T(1,128)S(1)}, f32[4,1,1280]{2,1,0:T(1,128)S(1)}, u32[]{:S(2)}, u32[]{:S(2)}) collective-permute-start(f32[4,1,1280]{2,1,0:T(1,128)S(1)} %get-tuple-element.157), channel_id=1, source_target_pairs={{1,0},{2,1},{3,2},{4,3},{5,4},{6,5},{7,6},{9,8},{10,9},{11,10},{12... | collective-permute-start | bytes 61448 | tf_op jit(solution)/shard_map/ppermute | solution.py:22
  33.6 6.6 %collective-permute-start.3 = (f32[4,1,1280]{2,1,0:T(1,128)S(1)}, f32[4,1,1280]{2,1,0:T(1,128)S(1)}, u32[]{:S(2)}, u32[]{:S(2)}) collective-permute-start(f32[4,1,1280]{2,1,0:T(1,128)S(1)} %get-tuple-element.158), channel_id=1, source_target_pairs={{0,1},{1,2},{2,3},{3,4},{4,5},{5,6},{6,7},{8,9},{9,10},{10,11},{11... | collective-permute-start | bytes 61448 | tf_op jit(solution)/shard_map/ppermute | solution.py:20
  42.1 13.9 %collective-permute-start.14 = (f32[2,4,1,1280]{3,2,1,0:T(1,128)S(1)}, f32[2,4,1,1280]{3,2,1,0:T(1,128)S(1)}, u32[]{:S(2)}, u32[]{:S(2)}) collective-permute-start(f32[2,4,1,1280]{3,2,1,0:T(1,128)S(1)} %get-tuple-element.109), channel_id=1, source_target_pairs={{0,1},{1,2},{2,3},{3,4},{4,5},{5,6},{6,7},{8,9},{9,10},{10,11},{11... | collective-permute-start | bytes 122888 | tf_op jit(solution)/shard_map/ppermute | solution.py:20
  46.9 9.1 %collective-permute-start.15 = (f32[2,4,1,1280]{3,2,1,0:T(1,128)S(1)}, f32[2,4,1,1280]{3,2,1,0:T(1,128)S(1)}, u32[]{:S(2)}, u32[]{:S(2)}) collective-permute-start(f32[2,4,1,1280]{3,2,1,0:T(1,128)S(1)} %get-tuple-element.110), channel_id=1, source_target_pairs={{1,0},{2,1},{3,2},{4,3},{5,4},{6,5},{7,6},{9,8},{10,9},{11,10},{12... | collective-permute-start | bytes 122888 | tf_op jit(solution)/shard_map/ppermute | solution.py:22
  48.3 7.9 %collective-permute-start.4 = (f32[4,1,1280]{2,1,0:T(1,128)S(1)}, f32[4,1,1280]{2,1,0:T(1,128)S(1)}, u32[]{:S(2)}, u32[]{:S(2)}) collective-permute-start(f32[4,1,1280]{2,1,0:T(1,128)S(1)} %get-tuple-element.151), channel_id=1, source_target_pairs={{1,0},{2,1},{3,2},{4,3},{5,4},{6,5},{7,6},{9,8},{10,9},{11,10},{12... | collective-permute-start | bytes 61448 | tf_op jit(solution)/shard_map/ppermute | solution.py:22
  49.6 7.8 %collective-permute-start.5 = (f32[4,1,1280]{2,1,0:T(1,128)S(1)}, f32[4,1,1280]{2,1,0:T(1,128)S(1)}, u32[]{:S(2)}, u32[]{:S(2)}) collective-permute-start(f32[4,1,1280]{2,1,0:T(1,128)S(1)} %get-tuple-element.152), channel_id=1, source_target_pairs={{0,1},{1,2},{2,3},{3,4},{4,5},{5,6},{6,7},{8,9},{9,10},{10,11},{11... | collective-permute-start | bytes 61448 | tf_op jit(solution)/shard_map/ppermute | solution.py:20
  59.3 13.9 %collective-permute-start.16 = (f32[2,4,1,1280]{3,2,1,0:T(1,128)S(1)}, f32[2,4,1,1280]{3,2,1,0:T(1,128)S(1)}, u32[]{:S(2)}, u32[]{:S(2)}) collective-permute-start(f32[2,4,1,1280]{3,2,1,0:T(1,128)S(1)} %get-tuple-element.107), channel_id=1, source_target_pairs={{0,1},{1,2},{2,3},{3,4},{4,5},{5,6},{6,7},{8,9},{9,10},{10,11},{11... | collective-permute-start | bytes 122888 | tf_op jit(solution)/shard_map/ppermute | solution.py:20
  64.1 9.1 %collective-permute-start.17 = (f32[2,4,1,1280]{3,2,1,0:T(1,128)S(1)}, f32[2,4,1,1280]{3,2,1,0:T(1,128)S(1)}, u32[]{:S(2)}, u32[]{:S(2)}) collective-permute-start(f32[2,4,1,1280]{3,2,1,0:T(1,128)S(1)} %get-tuple-element.108), channel_id=1, source_target_pairs={{1,0},{2,1},{3,2},{4,3},{5,4},{6,5},{7,6},{9,8},{10,9},{11,10},{12... | collective-permute-start | bytes 122888 | tf_op jit(solution)/shard_map/ppermute | solution.py:22
  65.5 7.9 %collective-permute-start.6 = (f32[4,1,1280]{2,1,0:T(1,128)S(1)}, f32[4,1,1280]{2,1,0:T(1,128)S(1)}, u32[]{:S(2)}, u32[]{:S(2)}) collective-permute-start(f32[4,1,1280]{2,1,0:T(1,128)S(1)} %get-tuple-element.145), channel_id=1, source_target_pairs={{1,0},{2,1},{3,2},{4,3},{5,4},{6,5},{7,6},{9,8},{10,9},{11,10},{12... | collective-permute-start | bytes 61448 | tf_op jit(solution)/shard_map/ppermute | solution.py:22
  66.8 7.8 %collective-permute-start.7 = (f32[4,1,1280]{2,1,0:T(1,128)S(1)}, f32[4,1,1280]{2,1,0:T(1,128)S(1)}, u32[]{:S(2)}, u32[]{:S(2)}) collective-permute-start(f32[4,1,1280]{2,1,0:T(1,128)S(1)} %get-tuple-element.146), channel_id=1, source_target_pairs={{0,1},{1,2},{2,3},{3,4},{4,5},{5,6},{6,7},{8,9},{9,10},{10,11},{11... | collective-permute-start | bytes 61448 | tf_op jit(solution)/shard_map/ppermute | solution.py:20
  75.7 1.7 copy-start.6
  75.7 3.9 %collective-permute-start.8 = (f32[4,16,1280]{2,1,0:T(8,128)S(1)}, f32[4,16,1280]{2,1,0:T(8,128)S(1)}, u32[]{:S(2)}, u32[]{:S(2)}) collective-permute-start(f32[4,16,1280]{2,1,0:T(8,128)S(1)} %get-tuple-element.28), channel_id=1, source_target_pairs={{0,8},{8,16},{16,24},{1,9},{9,17},{17,25},{2,10},{10,18},{18,26},{... | collective-permute-start | bytes 983048 | tf_op jit(solution)/shard_map/ppermute | solution.py:32
  77.4 2.2 copy-start.10
  77.4 2.2 copy-start.11
  79.6 1.0 copy-start.15
  134.1 6.5 %copy-start.12 = (f32[1,4,16,1280]{3,2,1,0:T(8,128)S(1)}, f32[1,4,16,1280]{3,2,1,0:T(8,128)}, u32[]{:S(2)}) copy-start(f32[1,4,16,1280]{3,2,1,0:T(8,128)} %param.7) | copy-start | bytes 983044
  134.2 6.5 %copy-start.16 = (f32[4,16,1280]{2,1,0:T(8,128)S(1)}, f32[4,16,1280]{2,1,0:T(8,128)}, u32[]{:S(2)}) copy-start(f32[4,16,1280]{2,1,0:T(8,128)} %copy-done.15) | copy-start | bytes 983044
  134.2 7.9 %copy-start.2 = (f32[1,4,4,16,1280]{4,3,2,1,0:T(8,128)S(1)}, f32[1,4,4,16,1280]{4,3,2,1,0:T(8,128)}, u32[]{:S(2)}) copy-start(f32[1,4,4,16,1280]{4,3,2,1,0:T(8,128)} %param.10) | copy-start | bytes 3932164
  134.4 7.7 %collective-permute-start.18 = (f32[4,1,1280]{2,1,0:T(1,128)S(1)}, f32[4,1,1280]{2,1,0:T(1,128)S(1)}, u32[]{:S(2)}, u32[]{:S(2)}) collective-permute-start(f32[4,1,1280]{2,1,0:T(1,128)S(1)} %get-tuple-element.137), channel_id=1, source_target_pairs={{1,0},{2,1},{3,2},{4,3},{5,4},{6,5},{7,6},{9,8},{10,9},{11,10},{12... | collective-permute-start | bytes 61448 | tf_op jit(solution)/shard_map/ppermute | solution.py:22
  135.8 6.3 %collective-permute-start.19 = (f32[4,1,1280]{2,1,0:T(1,128)S(1)}, f32[4,1,1280]{2,1,0:T(1,128)S(1)}, u32[]{:S(2)}, u32[]{:S(2)}) collective-permute-start(f32[4,1,1280]{2,1,0:T(1,128)S(1)} %get-tuple-element.138), channel_id=1, source_target_pairs={{0,1},{1,2},{2,3},{3,4},{4,5},{5,6},{6,7},{8,9},{9,10},{10,11},{11... | collective-permute-start | bytes 61448 | tf_op jit(solution)/shard_map/ppermute | solution.py:20
  140.7 78.3 %copy-start.13 = (f32[4,16,1280]{2,1,0:T(8,128)}, f32[4,16,1280]{2,1,0:T(8,128)S(1)}, u32[]{:S(2)}) copy-start(f32[4,16,1280]{2,1,0:T(8,128)S(1)} %multiply_subtract_fusion.1) | copy-start | bytes 983044
  140.8 31.3 %collective-permute-start.27 = (f32[4,16,1280]{2,1,0:T(8,128)S(1)}, f32[4,16,1280]{2,1,0:T(8,128)S(1)}, u32[]{:S(2)}, u32[]{:S(2)}) collective-permute-start(f32[4,16,1280]{2,1,0:T(8,128)S(1)} %multiply_subtract_fusion.1), channel_id=1, source_target_pairs={{8,0},{16,8},{24,16},{9,1},{17,9},{25,17},{10,2},{18,10},{26,18},{... | collective-permute-start | bytes 983048 | tf_op jit(solution)/shard_map/ppermute | solution.py:32
  142.7 6.8 %collective-permute-start.20 = (f32[4,1,1280]{2,1,0:T(1,128)S(1)}, f32[4,1,1280]{2,1,0:T(1,128)S(1)}, u32[]{:S(2)}, u32[]{:S(2)}) collective-permute-start(f32[4,1,1280]{2,1,0:T(1,128)S(1)} %get-tuple-element.131), channel_id=1, source_target_pairs={{1,0},{2,1},{3,2},{4,3},{5,4},{6,5},{7,6},{9,8},{10,9},{11,10},{12... | collective-permute-start | bytes 61448 | tf_op jit(solution)/shard_map/ppermute | solution.py:22
  144.0 6.9 %collective-permute-start.21 = (f32[4,1,1280]{2,1,0:T(1,128)S(1)}, f32[4,1,1280]{2,1,0:T(1,128)S(1)}, u32[]{:S(2)}, u32[]{:S(2)}) collective-permute-start(f32[4,1,1280]{2,1,0:T(1,128)S(1)} %get-tuple-element.132), channel_id=1, source_target_pairs={{0,1},{1,2},{2,3},{3,4},{4,5},{5,6},{6,7},{8,9},{9,10},{10,11},{11... | collective-permute-start | bytes 61448 | tf_op jit(solution)/shard_map/ppermute | solution.py:20
  151.4 7.1 %collective-permute-start.22 = (f32[4,1,1280]{2,1,0:T(1,128)S(1)}, f32[4,1,1280]{2,1,0:T(1,128)S(1)}, u32[]{:S(2)}, u32[]{:S(2)}) collective-permute-start(f32[4,1,1280]{2,1,0:T(1,128)S(1)} %get-tuple-element.125), channel_id=1, source_target_pairs={{1,0},{2,1},{3,2},{4,3},{5,4},{6,5},{7,6},{9,8},{10,9},{11,10},{12... | collective-permute-start | bytes 61448 | tf_op jit(solution)/shard_map/ppermute | solution.py:22
  152.7 7.2 %collective-permute-start.23 = (f32[4,1,1280]{2,1,0:T(1,128)S(1)}, f32[4,1,1280]{2,1,0:T(1,128)S(1)}, u32[]{:S(2)}, u32[]{:S(2)}) collective-permute-start(f32[4,1,1280]{2,1,0:T(1,128)S(1)} %get-tuple-element.126), channel_id=1, source_target_pairs={{0,1},{1,2},{2,3},{3,4},{4,5},{5,6},{6,7},{8,9},{9,10},{10,11},{11... | collective-permute-start | bytes 61448 | tf_op jit(solution)/shard_map/ppermute | solution.py:20
  160.2 9.2 %copy-start.9 = (f32[4,4,16,1280]{3,2,1,0:T(8,128)S(1)}, f32[4,4,16,1280]{3,2,1,0:T(8,128)}, u32[]{:S(2)}) copy-start(f32[4,4,16,1280]{3,2,1,0:T(8,128)} %get-tuple-element.51) | copy-start | bytes 3932164
  160.4 7.3 %collective-permute-start.24 = (f32[4,1,1280]{2,1,0:T(1,128)S(1)}, f32[4,1,1280]{2,1,0:T(1,128)S(1)}, u32[]{:S(2)}, u32[]{:S(2)}) collective-permute-start(f32[4,1,1280]{2,1,0:T(1,128)S(1)} %get-tuple-element.119), channel_id=1, source_target_pairs={{1,0},{2,1},{3,2},{4,3},{5,4},{6,5},{7,6},{9,8},{10,9},{11,10},{12... | collective-permute-start | bytes 61448 | tf_op jit(solution)/shard_map/ppermute | solution.py:22
  161.9 7.2 %collective-permute-start.25 = (f32[4,1,1280]{2,1,0:T(1,128)S(1)}, f32[4,1,1280]{2,1,0:T(1,128)S(1)}, u32[]{:S(2)}, u32[]{:S(2)}) collective-permute-start(f32[4,1,1280]{2,1,0:T(1,128)S(1)} %get-tuple-element.120), channel_id=1, source_target_pairs={{0,1},{1,2},{2,3},{3,4},{4,5},{5,6},{6,7},{8,9},{9,10},{10,11},{11... | collective-permute-start | bytes 61448 | tf_op jit(solution)/shard_map/ppermute | solution.py:20
  169.1 1.3 copy-start.4
  169.1 1.7 copy-start.7
  172.3 6.8 %collective-permute-start.28 = (f32[2,4,1,1280]{3,2,1,0:T(1,128)S(1)}, f32[2,4,1,1280]{3,2,1,0:T(1,128)S(1)}, u32[]{:S(2)}, u32[]{:S(2)}) collective-permute-start(f32[2,4,1,1280]{3,2,1,0:T(1,128)S(1)} %get-tuple-element.105), channel_id=1, source_target_pairs={{0,1},{1,2},{2,3},{3,4},{4,5},{5,6},{6,7},{8,9},{9,10},{10,11},{11... | collective-permute-start | bytes 122888 | tf_op jit(solution)/shard_map/ppermute | solution.py:20
  177.4 7.1 %collective-permute-start.29 = (f32[2,4,1,1280]{3,2,1,0:T(1,128)S(1)}, f32[2,4,1,1280]{3,2,1,0:T(1,128)S(1)}, u32[]{:S(2)}, u32[]{:S(2)}) collective-permute-start(f32[2,4,1,1280]{3,2,1,0:T(1,128)S(1)} %get-tuple-element.106), channel_id=1, source_target_pairs={{1,0},{2,1},{3,2},{4,3},{5,4},{6,5},{7,6},{9,8},{10,9},{11,10},{12... | collective-permute-start | bytes 122888 | tf_op jit(solution)/shard_map/ppermute | solution.py:22
  185.4 6.5 %collective-permute-start.30 = (f32[2,4,1,1280]{3,2,1,0:T(1,128)S(1)}, f32[2,4,1,1280]{3,2,1,0:T(1,128)S(1)}, u32[]{:S(2)}, u32[]{:S(2)}) collective-permute-start(f32[2,4,1,1280]{3,2,1,0:T(1,128)S(1)} %get-tuple-element.103), channel_id=1, source_target_pairs={{0,1},{1,2},{2,3},{3,4},{4,5},{5,6},{6,7},{8,9},{9,10},{10,11},{11... | collective-permute-start | bytes 122888 | tf_op jit(solution)/shard_map/ppermute | solution.py:20
  190.3 5.9 %collective-permute-start.31 = (f32[2,4,1,1280]{3,2,1,0:T(1,128)S(1)}, f32[2,4,1,1280]{3,2,1,0:T(1,128)S(1)}, u32[]{:S(2)}, u32[]{:S(2)}) collective-permute-start(f32[2,4,1,1280]{3,2,1,0:T(1,128)S(1)} %get-tuple-element.104), channel_id=1, source_target_pairs={{1,0},{2,1},{3,2},{4,3},{5,4},{6,5},{7,6},{9,8},{10,9},{11,10},{12... | collective-permute-start | bytes 122888 | tf_op jit(solution)/shard_map/ppermute | solution.py:22
  197.1 5.6 %collective-permute-start.32 = (f32[2,4,1,1280]{3,2,1,0:T(1,128)S(1)}, f32[2,4,1,1280]{3,2,1,0:T(1,128)S(1)}, u32[]{:S(2)}, u32[]{:S(2)}) collective-permute-start(f32[2,4,1,1280]{3,2,1,0:T(1,128)S(1)} %get-tuple-element.101), channel_id=1, source_target_pairs={{0,1},{1,2},{2,3},{3,4},{4,5},{5,6},{6,7},{8,9},{9,10},{10,11},{11... | collective-permute-start | bytes 122888 | tf_op jit(solution)/shard_map/ppermute | solution.py:20
  201.0 5.9 %collective-permute-start.33 = (f32[2,4,1,1280]{3,2,1,0:T(1,128)S(1)}, f32[2,4,1,1280]{3,2,1,0:T(1,128)S(1)}, u32[]{:S(2)}, u32[]{:S(2)}) collective-permute-start(f32[2,4,1,1280]{3,2,1,0:T(1,128)S(1)} %get-tuple-element.102), channel_id=1, source_target_pairs={{1,0},{2,1},{3,2},{4,3},{5,4},{6,5},{7,6},{9,8},{10,9},{11,10},{12... | collective-permute-start | bytes 122888 | tf_op jit(solution)/shard_map/ppermute | solution.py:22
  207.8 7.4 %collective-permute-start.34 = (f32[2,4,1,1280]{3,2,1,0:T(1,128)S(1)}, f32[2,4,1,1280]{3,2,1,0:T(1,128)S(1)}, u32[]{:S(2)}, u32[]{:S(2)}) collective-permute-start(f32[2,4,1,1280]{3,2,1,0:T(1,128)S(1)} %get-tuple-element.99), channel_id=1, source_target_pairs={{0,1},{1,2},{2,3},{3,4},{4,5},{5,6},{6,7},{8,9},{9,10},{10,11},{11... | collective-permute-start | bytes 122888 | tf_op jit(solution)/shard_map/ppermute | solution.py:20
  212.6 5.9 %collective-permute-start.35 = (f32[2,4,1,1280]{3,2,1,0:T(1,128)S(1)}, f32[2,4,1,1280]{3,2,1,0:T(1,128)S(1)}, u32[]{:S(2)}, u32[]{:S(2)}) collective-permute-start(f32[2,4,1,1280]{3,2,1,0:T(1,128)S(1)} %get-tuple-element.100), channel_id=1, source_target_pairs={{1,0},{2,1},{3,2},{4,3},{5,4},{6,5},{7,6},{9,8},{10,9},{11,10},{12... | collective-permute-start | bytes 122888 | tf_op jit(solution)/shard_map/ppermute | solution.py:22
  213.9 5.1 %collective-permute-start.26 = (f32[4,16,1280]{2,1,0:T(8,128)S(1)}, f32[4,16,1280]{2,1,0:T(8,128)S(1)}, u32[]{:S(2)}, u32[]{:S(2)}) collective-permute-start(f32[4,16,1280]{2,1,0:T(8,128)S(1)} %get-tuple-element.37), channel_id=1, source_target_pairs={{0,8},{8,16},{16,24},{1,9},{9,17},{17,25},{2,10},{10,18},{18,26},{... | collective-permute-start | bytes 983048 | tf_op jit(solution)/shard_map/ppermute | solution.py:32
  219.1 53.1 %copy-start.8 = (f32[1,4,4,16,1280]{4,3,2,1,0:T(8,128)S(1)}, f32[1,4,4,16,1280]{4,3,2,1,0:T(8,128)}, u32[]{:S(2)}) copy-start(f32[1,4,4,16,1280]{4,3,2,1,0:T(8,128)} %param.12) | copy-start | bytes 3932164
  220.2 52.0 %copy-start.5 = (f32[1,4,4,16,1280]{4,3,2,1,0:T(8,128)S(1)}, f32[1,4,4,16,1280]{4,3,2,1,0:T(8,128)}, u32[]{:S(2)}) copy-start(f32[1,4,4,16,1280]{4,3,2,1,0:T(8,128)} %param.8) | copy-start | bytes 3932164
  220.2 52.0 %copy-start.14 = (f32[1,1,4,16,1280]{4,3,2,1,0:T(8,128)S(1)}, f32[1,1,4,16,1280]{4,3,2,1,0:T(8,128)}, u32[]{:S(2)}) copy-start(f32[1,1,4,16,1280]{4,3,2,1,0:T(8,128)} %get-tuple-element.23) | copy-start | bytes 983044
where the time goes:
time: 276 us; the launch traced here: 275 us
  starting transfers between devices  109 us (39%)
  blocking collectives  93.2 us (34%)
  waiting for transfers between devices  30.9 us (11%)
  other arithmetic  22.3 us (8%)
  between operations  12 us (4%)
  local copies, waits for them, and re-layouts  6.98 us (3%)
    psum x2, blocking collectives, on_device(): inner, square = lax.psum((inner, square), ('tm', 'space'))  93.2 us
    ppermute x16, starting transfers between devices, extended(): lax.ppermute(tail, axis, [(i, (i + 1) % count) for i in range(ends)])  83 us
    ppermute x16, waiting for transfers between devices, extended(): lax.ppermute(head, axis, [((i + 1) % count, i) for i in range(ends)])  22.1 us
    ppermute x16, starting transfers between devices, extended(): lax.ppermute(head, axis, [((i + 1) % count, i) for i in range(ends)])  21.1 us
    ppermute x16, waiting for transfers between devices, extended(): lax.ppermute(tail, axis, [(i, (i + 1) % count) for i in range(ends)])  8.84 us
    reduce_sum x4, other arithmetic, on_device(): square = sum((jnp.sum(q * q) for q in image))  5.65 us
  transfers between devices with their start and end apart: 36, of which 15 were waited for; matrix products, arithmetic and copies ran while one was open for 3% of the time, Pallas kernels for 0%

commit v1 on v0

v1 whole, which is shorter than its diff:
```python
import functools

import jax
import jax.numpy as jnp
from jax import lax
from jax.experimental import pallas as pl
from jax.experimental.pallas import tpu as pltpu
from jax.sharding import PartitionSpec as P

KAPPA = 0.12
MESH = pl.DeviceIdType.MESH


def kernel(
    ntm, nsp,
    rs_h, ro_h, we_h, wn_h, mv_h, ov_h, mk_h,
    zdx_h, coef_ref,
    rs, ro, we, wn, mv, ov, mk,
    zl, zdx, u, t1, t2, st,
    lam_next, zl_next, u_next,
    acc, stage_lo, stage_hi, recv_lo, recv_hi,
    part, part_tm, part_sp,
    load_sem, slo_sem, shi_sem, rlo_sem, rhi_sem, tms_sem, tmr_sem,
    ptm_s, ptm_r, psp_s, psp_r, out_sem,
):
    steps, lev, rows, nlon = ro.shape
    last = rows - 1
    tm = lax.axis_index("tm")
    sp = lax.axis_index("space")
    has_lo, has_hi = sp > 0, sp < nsp - 1
    has_prev, has_next = tm > 0, tm < ntm - 1

    loads = {}

    def load(name, src, dst):
        copy = pltpu.make_async_copy(src, dst, load_sem.at[len(loads)])
        copy.start()
        loads[name] = copy

    load("rs", rs_h, rs)
    load("mv", mv_h, mv)
    for j in reversed(range(steps)):
        load(("mk", j), mk_h.at[j], mk.at[j])
        load(("ro", j), ro_h.at[j], ro.at[j])
        load(("wn", j), wn_h.at[j], wn.at[j])
        load(("we", j), we_h.at[j], we.at[j])
    for j in reversed(range(steps)):
        load(("ov", j), ov_h.at[j], ov.at[j])

    barrier = pltpu.get_barrier_semaphore()
    for d in range(1, ntm):
        pl.semaphore_signal(barrier, inc=1, device_id=(lax.rem(tm + d, ntm), sp), device_id_type=MESH)
    for d in range(1, nsp):
        pl.semaphore_signal(barrier, inc=1, device_id=(tm, lax.rem(sp + d, nsp)), device_id_type=MESH)
    pl.semaphore_wait(barrier, ntm + nsp - 2)

    def tm_copy(i, src, dst, device):
        return pltpu.make_async_remote_copy(
            src_ref=src, dst_ref=dst, send_sem=tms_sem.at[i], recv_sem=tmr_sem.at[i],
            device_id=(device, sp), device_id_type=MESH,
        )

    def tm_send(i, src, dst):
        @pl.when(has_prev)
        def _():
            tm_copy(i, src, dst, tm - 1).start()

    def tm_recv(i, src, dst):
        @pl.when(has_next)
        def _():
            tm_copy(i, src, dst, tm + 1).wait_recv()

    def to_lo(slot, device):
        return pltpu.make_async_remote_copy(
            src_ref=stage_lo.at[slot], dst_ref=recv_hi.at[slot],
            send_sem=slo_sem.at[slot], recv_sem=rhi_sem.at[slot],
            device_id=(tm, device), device_id_type=MESH,
        )

    def to_hi(slot, device):
        return pltpu.make_async_remote_copy(
            src_ref=stage_hi.at[slot], dst_ref=recv_lo.at[slot],
            send_sem=shi_sem.at[slot], recv_sem=rlo_sem.at[slot],
            device_id=(tm, device), device_id_type=MESH,
        )

    row = lax.broadcasted_iota(jnp.int32, (rows, nlon), 0)

    def down(x):
        return jnp.where(row == 0, 0.0, pltpu.roll(x, 1, 0))

    def up(x):
        return jnp.where(row == last, 0.0, pltpu.roll(x, rows - 1, 0))

    def before(x):
        return pltpu.roll(x, 1, 1)

    def after(x):
        return pltpu.roll(x, nlon - 1, 1)

    def fold(x):
        total = x[0:8]
        for i in range(8, rows, 8):
            total = total + x[i:i + 8]
        return total

    def levels(body):
        lax.fori_loop(0, lev, lambda l, c: (body(l), c)[1], 0)

    loads["rs"].wait()
    tm_send(0, rs, lam_next)
    loads["mv"].wait()

    def _(l):
        z = mv[l] * rs[l]
        zl[l] = z
        acc[0, l] = fold(z * rs[l])
        acc[1, l] = fold(z * z)
        acc[2, l] = jnp.zeros((8, nlon), jnp.float32)
        acc[3, l] = jnp.zeros((8, nlon), jnp.float32)
    levels(_)
    tm_send(1, zl, zl_next)

    @pl.when(jnp.logical_not(has_next))
    def _():
        lam_next[...] = jnp.zeros_like(lam_next)
        zl_next[...] = jnp.zeros_like(zl_next)

    def mask(j, l):
        return mk[j, l].astype(jnp.float32)

    for name in ("mk", "ro", "wn", "we"):
        loads[name, steps - 1].wait()
    tm_recv(0, rs, lam_next)

    def _(l):
        t1[l] = mask(steps - 1, l) * ro[steps - 1, l] - lam_next[l]
    levels(_)

    def send_adjoint(slot, t, j):
        def _(l):
            lo = t[l, 0:1, :]
            hi = t[l, last:rows, :]
            stage_lo[slot, pl.ds(l, 1), :] = KAPPA * lo + 0.5 * (wn[j, l, 0:1, :] * lo)
            stage_hi[slot, pl.ds(l, 1), :] = KAPPA * hi - 0.5 * (wn[j, l, last:rows, :] * hi)
        for l in range(lev):
            _(l)
        start(slot)

    def send_forward(slot, s):
        for l in range(lev):
            stage_lo[slot, pl.ds(l, 1), :] = s[l, 0:1, :]
            stage_hi[slot, pl.ds(l, 1), :] = s[l, last:rows, :]
        start(slot)

    def start(slot):
        @pl.when(has_lo)
        def _():
            to_lo(slot, sp - 1).start()

        @pl.when(has_hi)
        def _():
            to_hi(slot, sp + 1).start()

    def finish(slot, t, j=None):
        @pl.when(has_lo)
        def _():
            to_hi(slot, sp - 1).wait_recv()
            for l in range(lev):
                got = recv_lo[slot, pl.ds(l, 1), :]
                if j is not None:
                    got = (KAPPA + 0.5 * wn[j, l, 0:1, :]) * got
                t[l, 0:1, :] = t[l, 0:1, :] + got

        @pl.when(has_hi)
        def _():
            to_lo(slot, sp + 1).wait_recv()
            for l in range(lev):
                got = recv_hi[slot, pl.ds(l, 1), :]
                if j is not None:
                    got = (KAPPA - 0.5 * wn[j, l, last:rows, :]) * got
                t[l, last:rows, :] = t[l, last:rows, :] + got

    def transposed(t, j, l):
        x = t[l]
        k = KAPPA * x
        e = 0.5 * (we[j, l] * x)
        n = 0.5 * (wn[j, l] * x)
        return (1.0 - 4.0 * KAPPA) * x + before(k - e) + after(k + e) + down(k - n) + up(k + n)

    def adjoint1(j):
        if j > 0:
            def _(l):
                t1[l] = transposed(t1, j, l) + mask(j - 1, l) * ro[j - 1, l]
        else:
            def _(l):
                zdx[l] = transposed(t1, j, l) + rs[l]
        levels(_)

    def inject2(j, l):
        z = ov[j, l] * ro[j, l]
        acc[0, l] += fold(z * ro[j, l])
        acc[1, l] += fold(z * z)
        return mask(j, l) * z

    def adjoint2(j):
        if j > 0:
            def _(l):
                t2[l] = transposed(t2, j, l) + inject2(j - 1, l)
        else:
            def _(l):
                t2[l] = transposed(t2, j, l) + zl[l]
        levels(_)

    def observed(j, l, s):
        z = ov[j, l] * ro[j, l]
        w = ov[j, l] * z + mask(j, l) * s
        acc[2, l] += fold(z * w)
        acc[3, l] += fold(w * w)

    def forward(src, j):
        def _(l):
            x = src[l]
            if j > 0:
                observed(j - 1, l, x)
            else:
                acc[1, l] += fold(x * x)
                u[l] = mv[l] * zl[l] + x
            e, w = after(x), before(x)
            n, s = up(x), down(x)
            st[l] = (
                x
                - 0.5 * (we[j, l] * (e - w))
                - 0.5 * (wn[j, l] * (n - s))
                + KAPPA * (e + w + n + s - 4.0 * x)
            )
        levels(_)

    def start2():
        for j in reversed(range(steps)):
            loads["ov", j].wait()
        tm_recv(1, zl, zl_next)

        def _(l):
            t2[l] = inject2(steps - 1, l) - zl_next[l]
        levels(_)

    def round2(q):
        j = steps - 1 - q
        if q == 0:
            start2()
        else:
            finish(2 * steps + q - 1, t2)
        if q < steps:
            send_adjoint(2 * steps + q, t2, j)
            adjoint2(j)

    def own_window():
        @pl.when(jnp.logical_not(has_prev))
        def _():
            def _(l):
                acc[2, l] += fold(zl[l] * u[l])
                acc[3, l] += fold(u[l] * u[l])
            levels(_)

    def increments():
        def _(l):
            acc[2, l] += fold(zdx[l] * t2[l])
            acc[3, l] += fold(t2[l] * t2[l])
        levels(_)

    lag = steps // 2
    for r in range(2 * steps):
        if r < steps:
            j = steps - 1 - r
            send_adjoint(r, t1, j)
            if j > 0:
                for name in ("mk", "ro", "wn", "we"):
                    loads[name, j - 1].wait()
            adjoint1(j)
            target = t1 if j > 0 else zdx
            weight = None
        else:
            j = r - steps
            src = zdx if j == 0 else st
            send_forward(r, src)
            if j == 0:
                out = pltpu.make_async_copy(zdx, zdx_h, out_sem)
                out.start()
            forward(src, j)
            if j == 0:
                tm_send(2, u, u_next)
            target, weight = st, j
        if lag <= r <= lag + steps:
            round2(r - lag)
        if r == lag + steps:
            increments()
        if r == 2 * steps - 1:
            own_window()
            tm_recv(2, u, u_next)
        finish(r, target, weight)

    def _(l):
        observed(steps - 1, l, st[l])
    levels(_)

    @pl.when(has_next)
    def _():
        def _(l):
            w = u_next[l] - st[l]
            acc[2, l] += fold(zl_next[l] * w)
            acc[3, l] += fold(w * w)
        levels(_)

    for i in range(4):
        total = acc[i, 0]
        for l in range(1, lev):
            total = total + acc[i, l]
        lanes = total[:, 0:128]
        for c in range(128, nlon, 128):
            lanes = lanes + total[:, c:c + 128]
        part[0, i:i + 1, :] = jnp.sum(lanes, axis=0, keepdims=True)
    part[0, 4:8, :] = jnp.zeros((4, 128), jnp.float32)

    def gather(count, slots, sends, recvs, device, src):
        copies = [
            pltpu.make_async_remote_copy(
                src_ref=src, dst_ref=slots.at[d - 1],
                send_sem=sends.at[d - 1], recv_sem=recvs.at[d - 1],
                device_id=device(d), device_id_type=MESH,
            )
            for d in range(1, count)
        ]
        for copy in copies:
            copy.start()
        total = src[...]
        for d, copy in enumerate(copies):
            copy.wait_recv()
            total = total + slots[d]
        return total, copies

    total, copies1 = gather(
        ntm, part_tm, ptm_s, ptm_r, lambda d: (lax.rem(tm + d, ntm), sp), part.at[0]
    )
    part[1] = total
    total, copies2 = gather(
        nsp, part_sp, psp_s, psp_r, lambda d: (tm, lax.rem(sp + d, nsp)), part.at[1]
    )
    sums = jnp.broadcast_to(jnp.sum(total, axis=1, keepdims=True), (8, 128))
    n, d, e, f = (sums[i:i + 1, :] for i in range(4))
    first = n / d
    second = first * (first * e - d) / (d - 2.0 * first * e + first * first * f)
    coef_ref[0:1, :] = first + second
    coef_ref[1:2, :] = -(first * second)
    coef_ref[2:8, :] = jnp.zeros((6, 128), jnp.float32)

    for copy in copies1 + copies2:
        copy.wait_send()
    for slot in range(3 * steps):
        @pl.when(has_lo)
        def _(slot=slot):
            to_lo(slot, sp - 1).wait_send()

        @pl.when(has_hi)
        def _(slot=slot):
            to_hi(slot, sp + 1).wait_send()

    @pl.when(has_prev)
    def _():
        tm_copy(0, rs, lam_next, tm - 1).wait_send()
        tm_copy(1, zl, zl_next, tm - 1).wait_send()
        tm_copy(2, u, u_next, tm - 1).wait_send()
    out.wait()


def on_device(ntm, nsp, *args):
    rhs_state, rhs_obs, wind_east, wind_north, model_var, obs_var, obs_mask = (a[0] for a in args)
    steps, lev, rows, nlon = rhs_obs.shape
    f32 = jnp.float32
    field = pltpu.VMEM((lev, rows, nlon), f32)
    fields = pltpu.VMEM((steps, lev, rows, nlon), f32)
    slots = 3 * steps
    halo = pltpu.VMEM((slots, lev, nlon), f32)
    dma = pltpu.SemaphoreType.DMA
    hbm = pl.BlockSpec(memory_space=pl.ANY)
    zdx, coef = pl.pallas_call(
        functools.partial(kernel, ntm, nsp),
        out_shape=(
            jax.ShapeDtypeStruct((lev, rows, nlon), f32),
            jax.ShapeDtypeStruct((8, 128), f32),
        ),
        in_specs=[hbm] * 7,
        out_specs=(hbm, pl.BlockSpec(memory_space=pltpu.VMEM)),
        scratch_shapes=[
            field, fields, fields, fields, field, fields,
            pltpu.VMEM((steps, lev, rows, nlon), jnp.int32),
            field, field, field, field, field, field,
            field, field, field,
            pltpu.VMEM((4, lev, 8, nlon), f32), halo, halo, halo, halo,
            pltpu.VMEM((2, 8, 128), f32),
            pltpu.VMEM((ntm - 1, 8, 128), f32),
            pltpu.VMEM((nsp - 1, 8, 128), f32),
            dma((2 + 5 * steps,)), dma((slots,)), dma((slots,)), dma((slots,)), dma((slots,)),
            dma((3,)), dma((3,)),
            dma((ntm - 1,)), dma((ntm - 1,)), dma((nsp - 1,)), dma((nsp - 1,)), dma,
        ],
        compiler_params=pltpu.CompilerParams(
            collective_id=0, has_side_effects=True, vmem_limit_bytes=56 * 1024 * 1024
        ),
    )(rhs_state, rhs_obs, wind_east, wind_north, model_var, obs_var, obs_mask)
    both, cross = coef[0, 0], coef[1, 0]
    return (
        ((both + cross * model_var) * rhs_state)[None],
        ((both + cross * obs_var) * rhs_obs)[None],
        (cross * zdx)[None],
    )


def solution(mesh):
    flat = P("tm", None, "space", None)
    deep = P("tm", None, None, "space", None)
    return jax.shard_map(
        functools.partial(on_device, mesh.shape["tm"], mesh.shape["space"]),
        mesh=mesh,
        in_specs=(flat, deep, deep, deep, flat, deep, deep),
        out_specs=(flat, deep, flat),
        check_vma=False,
    )
```

time: 276 us -> 51.2 us (0.19)
  starting transfers between devices: 109 us -> 0 us
  blocking collectives: 93.2 us -> 0 us
  Pallas kernels: 0 us -> 42.1 us
  waiting for transfers between devices: 30.9 us -> 0 us
  other arithmetic: 22.3 us -> 6.87 us
  between operations: 12 us -> 0.68 us
  local copies, waits for them, and re-layouts: 6.98 us -> 1.39 us
    ppermute x36 -> x0, starting transfers between devices: 109 us -> none  [the longest x16 83 us: extended(): lax.ppermute(tail, axis, [(i, (i + 1) % count) for i in range(ends)])]
    psum x2 -> x0, blocking collectives: 93.2 us -> none  [on_device(): inner, square = lax.psum((inner, square), ('tm', 'space'))]
    pallas_call x0 -> x1, Pallas kernels: none -> 42.1 us  [on_device(): pl.pallas_call(functools.partial(kernel, ntm, nsp), out_shape=(jax.ShapeD...]
    ppermute x36 -> x0, waiting for transfers between devices: 30.9 us -> none  [the longest x16 22.1 us: extended(): lax.ppermute(head, axis, [((i + 1) % count, i) for i in range(ends)])]
    another operation x16 -> x0, other arithmetic: 8.34 us -> none  [the longest x8 4.61 us: forward(): return (current, jnp.stack(observed, 0))]
    reduce_sum x4 -> x0, other arithmetic: 5.65 us -> none  [on_device(): square = sum((jnp.sum(q * q) for q in image))]
    mul x1 -> x2, other arithmetic: 0.01 us -> 4.48 us  [the longest x1 2.48 us: on_device(): (both + cross * obs_var) * rhs_obs]
    unnamed x34 -> x8, local copies, waits for them, and re-layouts: 2.9 us -> 0.02 us
  transfers between devices with their start and end apart: 36 -> 0, of which waited for: 15 -> 0; matrix products, arithmetic and copies ran while one was open for 3% -> 0% of each run, Pallas kernels for 0% -> 0%
where the time goes in v1:
time: 51.2 us; the launch traced here: 51 us
  Pallas kernels  42.1 us (82%)
  other arithmetic  6.87 us (13%)
  local copies, waits for them, and re-layouts  1.39 us (3%)
  between operations  0.68 us (1%)
    pallas_call x1, Pallas kernels, on_device(): pl.pallas_call(functools.partial(kernel, ntm, nsp), out_shape=(jax.ShapeD...  42.1 us
    mul x1, other arithmetic, on_device(): (both + cross * obs_var) * rhs_obs  2.48 us
    broadcast_in_dim x1, other arithmetic, on_device(): (cross * zdx)[None]  2.39 us
    mul x1, other arithmetic, on_device(): (both + cross * model_var) * rhs_state  2 us
    slice x1, local copies, waits for them, and re-layouts, on_device(): both, cross = (coef[0, 0], coef[1, 0])  1.37 us

profile of v1, /device:TPU:0, one launch (start us, length us, event | category | flops | bytes accessed | tf_op | source)
XLA Modules:
  0.0 51.0 jit_solution(5140956268709556990)
XLA Ops:
  0.6 0.0 copy-start.2
  0.6 0.0 copy-start.3
  0.7 0.0 copy-start.1
  0.7 42.1 %shard_map.94 = (f32[4,16,1280]{2,1,0:T(8,128)}, f32[8,128]{1,0:T(8,128)}) custom-call(f32[4,16,1280]{2,1,0:T(8,128)} %bitcast.13, f32[4,4,16,1280]{3,2,1,0:T(8,128)} %bitcast.11, f32[4,4,16,1280]{3,2,1,0:T(8,128)} %bitcast.15, f32[4,4,16,1280]{3,2,1,0:T(8,128)} %bitcast.16, f32[4,16,1280]{2,1,0:T(8,128)} %bitcast.14, f32[4,4,16,1280]{3,2,1,0:T(8,128)} %bitcast.12, ...), custom_call_target="tpu_custom_call" | custom-call | tf_op jit(solution)/shard_map/pallas_call | solution.py:386
  42.8 0.0 copy-start
  42.8 1.4 %fusion = (f32[1,1]{1,0:T(1,128)}, f32[1,1]{1,0:T(1,128)}) fusion(f32[8,128]{1,0:T(8,128)} %get-tuple-element.5), kind=kLoop, calls=%fused_computation.3 | loop fusion | bytes 16 | tf_op jit(solution)/shard_map/slice | solution.py:411
  44.1 2.4 %multiply_bitcast_fusion = f32[1,4,16,1280]{3,2,1,0:T(8,128)} fusion(f32[4,16,1280]{2,1,0:T(8,128)} %get-tuple-element.6, f32[]{:T(128)} %bitcast.8), kind=kLoop, calls=%fused_computation.1 | loop fusion | flops 81920 | bytes 655364 | tf_op jit(solution)/shard_map/broadcast_in_dim | solution.py:415
  46.5 0.0 copy-done.2
  46.5 0.0 copy-done.3
  46.5 2.0 %add_multiply_fusion.1 = f32[1,4,16,1280]{3,2,1,0:T(8,128)} fusion(f32[1,4,16,1280]{3,2,1,0:T(8,128)S(1)} %copy-done.2, f32[1,4,16,1280]{3,2,1,0:T(8,128)S(1)} %copy-done.3, f32[]{:T(128)} %bitcast.8, f32[]{:T(128)} %bitcast.7), kind=kLoop, calls=%fused_computation.2 | loop fusion | flops 245760 | bytes 983048 | tf_op jit(solution)/shard_map/mul | solution.py:413
  48.5 0.0 copy-done.1
  48.5 0.0 copy-done
  48.5 2.5 %add_multiply_fusion = f32[1,4,4,16,1280]{4,3,2,1,0:T(8,128)} fusion(f32[1,4,4,16,1280]{4,3,2,1,0:T(8,128)S(1)} %copy-done, f32[1,4,4,16,1280]{4,3,2,1,0:T(8,128)S(1)} %copy-done.1, f32[]{:T(128)} %bitcast.8, f32[]{:T(128)} %bitcast.7), kind=kLoop, calls=%fused_computation | loop fusion | flops 983040 | bytes 3932168 | tf_op jit(solution)/shard_map/mul | solution.py:414
Async XLA Ops:
  0.6 45.9 %copy-start.2 = (f32[1,4,16,1280]{3,2,1,0:T(8,128)S(1)}, f32[1,4,16,1280]{3,2,1,0:T(8,128)}, u32[]{:S(2)}) copy-start(f32[1,4,16,1280]{3,2,1,0:T(8,128)} %param.7) | copy-start | bytes 983044
  0.6 45.9 %copy-start.3 = (f32[1,4,16,1280]{3,2,1,0:T(8,128)S(1)}, f32[1,4,16,1280]{3,2,1,0:T(8,128)}, u32[]{:S(2)}) copy-start(f32[1,4,16,1280]{3,2,1,0:T(8,128)} %param.11) | copy-start | bytes 983044
  0.7 47.9 %copy-start.1 = (f32[1,4,4,16,1280]{4,3,2,1,0:T(8,128)S(1)}, f32[1,4,4,16,1280]{4,3,2,1,0:T(8,128)}, u32[]{:S(2)}) copy-start(f32[1,4,4,16,1280]{4,3,2,1,0:T(8,128)} %param.12) | copy-start | bytes 3932164
  42.8 5.8 %copy-start = (f32[1,4,4,16,1280]{4,3,2,1,0:T(8,128)S(1)}, f32[1,4,4,16,1280]{4,3,2,1,0:T(8,128)}, u32[]{:S(2)}) copy-start(f32[1,4,4,16,1280]{4,3,2,1,0:T(8,128)} %param.8) | copy-start | bytes 3932164

commit v2 on v1

--- a/solution.py
+++ b/solution.py
@@ -371,6 +371,34 @@
         tm_copy(1, zl, zl_next, tm - 1).wait_send()
         tm_copy(2, u, u_next, tm - 1).wait_send()
     out.wait()
+
+
+def combine(coef, rs, ro, mv, ov, zdx, lam_h, mu_h, dx_h, lam, mu, dx, sem):
+    steps, lev, rows, nlon = ro.shape
+    both = jnp.broadcast_to(coef[0:1, 0:1], (rows, nlon))
+    cross = jnp.broadcast_to(coef[1:2, 0:1], (rows, nlon))
+    copies = []
+
+    def put(body, src, dst):
+        lax.fori_loop(0, lev, lambda l, c: (body(l), c)[1], 0)
+        copy = pltpu.make_async_copy(src, dst, sem.at[len(copies)])
+        copy.start()
+        copies.append(copy)
+
+    for j in range(steps):
+        def _(l, j=j):
+            mu[j, l] = (both + cross * ov[j, l]) * ro[j, l]
+        put(_, mu.at[j], mu_h.at[j])
+
+    def _(l):
+        lam[l] = (both + cross * mv[l]) * rs[l]
+    put(_, lam, lam_h)
+
+    def _(l):
+        dx[l] = cross * zdx[l]
+    put(_, dx, dx_h)
+    for copy in copies:
+        copy.wait()
 
 
 def on_device(ntm, nsp, *args):
@@ -405,15 +433,23 @@
             dma((ntm - 1,)), dma((ntm - 1,)), dma((nsp - 1,)), dma((nsp - 1,)), dma,
         ],
         compiler_params=pltpu.CompilerParams(
-            collective_id=0, has_side_effects=True, vmem_limit_bytes=56 * 1024 * 1024
+            collective_id=0, has_side_effects=True, vmem_limit_bytes=52 * 1024 * 1024
         ),
     )(rhs_state, rhs_obs, wind_east, wind_north, model_var, obs_var, obs_mask)
-    both, cross = coef[0, 0], coef[1, 0]
-    return (
-        ((both + cross * model_var) * rhs_state)[None],
-        ((both + cross * obs_var) * rhs_obs)[None],
-        (cross * zdx)[None],
-    )
+    vmem = pl.BlockSpec(memory_space=pltpu.VMEM)
+    lam, mu, dx = pl.pallas_call(
+        combine,
+        out_shape=(
+            jax.ShapeDtypeStruct((lev, rows, nlon), f32),
+            jax.ShapeDtypeStruct((steps, lev, rows, nlon), f32),
+            jax.ShapeDtypeStruct((lev, rows, nlon), f32),
+        ),
+        in_specs=[vmem] * 6,
+        out_specs=(hbm, hbm, hbm),
+        scratch_shapes=[field, fields, field, dma((steps + 2,))],
+        compiler_params=pltpu.CompilerParams(vmem_limit_bytes=16 * 1024 * 1024),
+    )(coef, rhs_state, rhs_obs, model_var, obs_var, zdx)
+    return lam[None], mu[None], dx[None]
 
 
 def solution(mesh):

time: 51.2 us -> 45.9 us (0.90)
  other arithmetic: 6.87 us -> 0 us
  Pallas kernels: 42.1 us -> 43.1 us
  local copies, waits for them, and re-layouts: 1.39 us -> 1.95 us
    mul x2 -> x0, other arithmetic: 4.48 us -> none  [the longest x1 2.48 us: on_device(): (both + cross * obs_var) * rhs_obs]
    broadcast_in_dim x1 -> x0, other arithmetic: 2.39 us -> none  [on_device(): (cross * zdx)[None]]
    unnamed x8, local copies, waits for them, and re-layouts: 0.02 us -> 1.95 us
    pallas_call x0 -> x1, Pallas kernels: none -> 1.4 us  [on_device(): pl.pallas_call(combine, out_shape=(jax.ShapeDtypeStruct((lev, rows, nlon)...]
    slice x1 -> x0, local copies, waits for them, and re-layouts: 1.37 us -> none  [on_device(): both, cross = (coef[0, 0], coef[1, 0])]
where the time goes in v2:
time: 45.9 us; the launch traced here: 45.7 us
  Pallas kernels  43.1 us (94%)
  local copies, waits for them, and re-layouts  1.95 us (4%)
  between operations  0.67 us (1%)
    pallas_call x1, Pallas kernels, on_device(): pl.pallas_call(functools.partial(kernel, ntm, nsp), out_shape=(jax.ShapeD...  41.7 us
    unnamed x8, local copies, waits for them, and re-layouts  1.95 us
    pallas_call x1, Pallas kernels, on_device(): pl.pallas_call(combine, out_shape=(jax.ShapeDtypeStruct((lev, rows, nlon)...  1.4 us

profile of v2, /device:TPU:0, one launch (start us, length us, event | category | flops | bytes accessed | tf_op | source)
XLA Modules:
  0.0 45.7 jit_solution(3857042601118626585)
XLA Ops:
  0.6 0.0 copy-start.2
  0.6 1.0 %copy-done.2 = f32[1,4,16,1280]{3,2,1,0:T(8,128)S(1)} copy-done((f32[1,4,16,1280]{3,2,1,0:T(8,128)S(1)}, f32[1,4,16,1280]{3,2,1,0:T(8,128)}, u32[]{:S(2)}) %copy-start.2) | copy-done | bytes 327704
  1.6 0.0 copy-start.3
  1.6 1.0 %copy-done.3 = f32[1,4,16,1280]{3,2,1,0:T(8,128)S(1)} copy-done((f32[1,4,16,1280]{3,2,1,0:T(8,128)S(1)}, f32[1,4,16,1280]{3,2,1,0:T(8,128)}, u32[]{:S(2)}) %copy-start.3) | copy-done | bytes 327704
  2.6 0.0 copy-start
  2.6 0.0 copy-start.1
  2.6 41.7 %shard_map.94 = (f32[4,16,1280]{2,1,0:T(8,128)S(1)}, f32[8,128]{1,0:T(8,128)S(1)}) custom-call(f32[4,16,1280]{2,1,0:T(8,128)S(1)} %bitcast.14, f32[4,4,16,1280]{3,2,1,0:T(8,128)} %bitcast.10, f32[4,4,16,1280]{3,2,1,0:T(8,128)} %bitcast.18, f32[4,4,16,1280]{3,2,1,0:T(8,128)} %bitcast.19, f32[4,16,1280]{2,1,0:T(8,128)S(1)} %bitcast.16, ...), custom_call_target="tpu_custom_call" | custom-call | tf_op jit(solution)/shard_map/pallas_call | solution.py:414
  44.2 0.0 copy-done
  44.3 0.0 copy-done.1
  44.3 1.4 %shard_map.95 = (f32[4,16,1280]{2,1,0:T(8,128)}, f32[4,4,16,1280]{3,2,1,0:T(8,128)}, f32[4,16,1280]{2,1,0:T(8,128)}) custom-call(f32[8,128]{1,0:T(8,128)S(1)} %get-tuple-element.8.coef, f32[4,16,1280]{2,1,0:T(8,128)S(1)} %bitcast.15, f32[4,4,16,1280]{3,2,1,0:T(8,128)S(1)} %bitcast.11, f32[4,16,1280]{2,1,0:T(8,128)S(1)} %bitcast.17, ...), custom_call_target="tpu_custom_call" | custom-call | tf_op jit(solution)/shard_map/pallas_call | solution.py:440
Async XLA Ops:
  0.6 1.0 %copy-start.2 = (f32[1,4,16,1280]{3,2,1,0:T(8,128)S(1)}, f32[1,4,16,1280]{3,2,1,0:T(8,128)}, u32[]{:S(2)}) copy-start(f32[1,4,16,1280]{3,2,1,0:T(8,128)} %param.7) | copy-start | bytes 983044
  1.6 1.0 %copy-start.3 = (f32[1,4,16,1280]{3,2,1,0:T(8,128)S(1)}, f32[1,4,16,1280]{3,2,1,0:T(8,128)}, u32[]{:S(2)}) copy-start(f32[1,4,16,1280]{3,2,1,0:T(8,128)} %param.11) | copy-start | bytes 983044
  2.6 41.7 %copy-start = (f32[1,4,4,16,1280]{4,3,2,1,0:T(8,128)S(1)}, f32[1,4,4,16,1280]{4,3,2,1,0:T(8,128)}, u32[]{:S(2)}) copy-start(f32[1,4,4,16,1280]{4,3,2,1,0:T(8,128)} %param.8) | copy-start | bytes 3932164
  2.6 41.7 %copy-start.1 = (f32[1,4,4,16,1280]{4,3,2,1,0:T(8,128)S(1)}, f32[1,4,4,16,1280]{4,3,2,1,0:T(8,128)}, u32[]{:S(2)}) copy-start(f32[1,4,4,16,1280]{4,3,2,1,0:T(8,128)} %param.12) | copy-start | bytes 3932164

commit v3 on v2

--- a/solution.py
+++ b/solution.py
@@ -17,7 +17,7 @@
     zdx_h, coef_ref,
     rs, ro, we, wn, mv, ov, mk,
     zl, zdx, u, t1, t2, st,
-    lam_next, zl_next, u_next,
+    lam_next, zl_next, u_next, rim, rim_next,
     acc, stage_lo, stage_hi, recv_lo, recv_hi,
     part, part_tm, part_sp,
     load_sem, slo_sem, shi_sem, rlo_sem, rhi_sem, tms_sem, tmr_sem,
@@ -108,6 +108,10 @@
         lax.fori_loop(0, lev, lambda l, c: (body(l), c)[1], 0)
 
     loads["rs"].wait()
+    for l in range(lev):
+        rim[0, l:l + 1, :] = rs[l, 0:1, :]
+        rim[1, l:l + 1, :] = rs[l, last:rows, :]
+    tm_send(3, rim, rim_next)
     tm_send(0, rs, lam_next)
     loads["mv"].wait()
 
@@ -123,6 +127,7 @@
 
     @pl.when(jnp.logical_not(has_next))
     def _():
+        rim_next[...] = jnp.zeros_like(rim_next)
         lam_next[...] = jnp.zeros_like(lam_next)
         zl_next[...] = jnp.zeros_like(zl_next)
 
@@ -131,16 +136,17 @@
 
     for name in ("mk", "ro", "wn", "we"):
         loads[name, steps - 1].wait()
-    tm_recv(0, rs, lam_next)
-
-    def _(l):
-        t1[l] = mask(steps - 1, l) * ro[steps - 1, l] - lam_next[l]
-    levels(_)
+    def first_row(side, i, l):
+        j = steps - 1
+        seen = mk[j, l, i:i + 1, :].astype(jnp.float32)
+        return seen * ro[j, l, i:i + 1, :] - rim_next[side, l:l + 1, :]
 
     def send_adjoint(slot, t, j):
         def _(l):
-            lo = t[l, 0:1, :]
-            hi = t[l, last:rows, :]
+            if slot == 0:
+                lo, hi = first_row(0, 0, l), first_row(1, last, l)
+            else:
+                lo, hi = t[l, 0:1, :], t[l, last:rows, :]
             stage_lo[slot, pl.ds(l, 1), :] = KAPPA * lo + 0.5 * (wn[j, l, 0:1, :] * lo)
             stage_hi[slot, pl.ds(l, 1), :] = KAPPA * hi - 0.5 * (wn[j, l, last:rows, :] * hi)
         for l in range(lev):
@@ -273,7 +279,15 @@
     for r in range(2 * steps):
         if r < steps:
             j = steps - 1 - r
+            if r == 0:
+                tm_recv(3, rim, rim_next)
             send_adjoint(r, t1, j)
+            if r == 0:
+                tm_recv(0, rs, lam_next)
+
+                def _(l):
+                    t1[l] = mask(steps - 1, l) * ro[steps - 1, l] - lam_next[l]
+                levels(_)
             if j > 0:
                 for name in ("mk", "ro", "wn", "we"):
                     loads[name, j - 1].wait()
@@ -367,13 +381,19 @@
 
     @pl.when(has_prev)
     def _():
+        tm_copy(3, rim, rim_next, tm - 1).wait_send()
         tm_copy(0, rs, lam_next, tm - 1).wait_send()
         tm_copy(1, zl, zl_next, tm - 1).wait_send()
         tm_copy(2, u, u_next, tm - 1).wait_send()
     out.wait()
 
 
-def combine(coef, rs, ro, mv, ov, zdx, lam_h, mu_h, dx_h, lam, mu, dx, sem):
+def combine(coef_h, zdx_h, rs, ro, mv, ov, lam_h, mu_h, dx_h, lam, mu, dx, coef, zdx, sem, in_sem):
+    get_coef = pltpu.make_async_copy(coef_h, coef, in_sem.at[0])
+    get_zdx = pltpu.make_async_copy(zdx_h, zdx, in_sem.at[1])
+    get_coef.start()
+    get_zdx.start()
+    get_coef.wait()
     steps, lev, rows, nlon = ro.shape
     both = jnp.broadcast_to(coef[0:1, 0:1], (rows, nlon))
     cross = jnp.broadcast_to(coef[1:2, 0:1], (rows, nlon))
@@ -393,6 +413,8 @@
     def _(l):
         lam[l] = (both + cross * mv[l]) * rs[l]
     put(_, lam, lam_h)
+
+    get_zdx.wait()
 
     def _(l):
         dx[l] = cross * zdx[l]
@@ -409,6 +431,7 @@
     fields = pltpu.VMEM((steps, lev, rows, nlon), f32)
     slots = 3 * steps
     halo = pltpu.VMEM((slots, lev, nlon), f32)
+    rim = pltpu.VMEM((2, lev, nlon), f32)
     dma = pltpu.SemaphoreType.DMA
     hbm = pl.BlockSpec(memory_space=pl.ANY)
     zdx, coef = pl.pallas_call(
@@ -423,17 +446,17 @@
             field, fields, fields, fields, field, fields,
             pltpu.VMEM((steps, lev, rows, nlon), jnp.int32),
             field, field, field, field, field, field,
-            field, field, field,
+            field, field, field, rim, rim,
             pltpu.VMEM((4, lev, 8, nlon), f32), halo, halo, halo, halo,
             pltpu.VMEM((2, 8, 128), f32),
             pltpu.VMEM((ntm - 1, 8, 128), f32),
             pltpu.VMEM((nsp - 1, 8, 128), f32),
             dma((2 + 5 * steps,)), dma((slots,)), dma((slots,)), dma((slots,)), dma((slots,)),
-            dma((3,)), dma((3,)),
+            dma((4,)), dma((4,)),
             dma((ntm - 1,)), dma((ntm - 1,)), dma((nsp - 1,)), dma((nsp - 1,)), dma,
         ],
         compiler_params=pltpu.CompilerParams(
-            collective_id=0, has_side_effects=True, vmem_limit_bytes=52 * 1024 * 1024
+            collective_id=0, has_side_effects=True, vmem_limit_bytes=56 * 1024 * 1024
         ),
     )(rhs_state, rhs_obs, wind_east, wind_north, model_var, obs_var, obs_mask)
     vmem = pl.BlockSpec(memory_space=pltpu.VMEM)
@@ -444,11 +467,13 @@
             jax.ShapeDtypeStruct((steps, lev, rows, nlon), f32),
             jax.ShapeDtypeStruct((lev, rows, nlon), f32),
         ),
-        in_specs=[vmem] * 6,
+        in_specs=[hbm] * 2 + [vmem] * 4,
         out_specs=(hbm, hbm, hbm),
-        scratch_shapes=[field, fields, field, dma((steps + 2,))],
+        scratch_shapes=[
+            field, fields, field, pltpu.VMEM((8, 128), f32), field, dma((steps + 2,)), dma((2,)),
+        ],
         compiler_params=pltpu.CompilerParams(vmem_limit_bytes=16 * 1024 * 1024),
-    )(coef, rhs_state, rhs_obs, model_var, obs_var, zdx)
+    )(coef, zdx, rhs_state, rhs_obs, model_var, obs_var)
     return lam[None], mu[None], dx[None]
 
 

time: 45.9 us -> 45.2 us (0.985)
    pallas_call x1, Pallas kernels: 41.7 us -> 41.2 us  [on_device(): pl.pallas_call(functools.partial(kernel, ntm, nsp), out_shape=(jax.ShapeD...]
    unnamed x8 -> x12, local copies, waits for them, and re-layouts: 1.95 us -> 1.66 us
where the time goes in v3:
time: 45.2 us; the launch traced here: 45 us
  Pallas kernels  42.7 us (94%)
  local copies, waits for them, and re-layouts  1.66 us (4%)
  between operations  0.71 us (2%)
    pallas_call x1, Pallas kernels, on_device(): pl.pallas_call(functools.partial(kernel, ntm, nsp), out_shape=(jax.ShapeD...  41.2 us
    unnamed x12, local copies, waits for them, and re-layouts  1.66 us
    pallas_call x1, Pallas kernels, on_device(): pl.pallas_call(combine, out_shape=(jax.ShapeDtypeStruct((lev, rows, nlon)...  1.52 us

profile of v3, /device:TPU:0, one launch (start us, length us, event | category | flops | bytes accessed | tf_op | source)
XLA Modules:
  0.0 45.0 jit_solution(9300433757109734495)
XLA Ops:
  0.6 0.0 copy-start
  0.6 0.0 copy-start.1
  0.7 0.0 copy-start.2
  0.7 0.0 copy-start.3
  0.7 41.2 %shard_map.94 = (f32[4,16,1280]{2,1,0:T(8,128)}, f32[8,128]{1,0:T(8,128)}) custom-call(f32[4,16,1280]{2,1,0:T(8,128)} %bitcast.14, f32[4,4,16,1280]{3,2,1,0:T(8,128)} %bitcast.10, f32[4,4,16,1280]{3,2,1,0:T(8,128)} %bitcast.18, f32[4,4,16,1280]{3,2,1,0:T(8,128)} %bitcast.19, f32[4,16,1280]{2,1,0:T(8,128)} %bitcast.16, f32[4,4,16,1280]{3,2,1,0:T(8,128)} %bitcast.12, ...), custom_call_target="tpu_custom_call" | custom-call | tf_op jit(solution)/shard_map/pallas_call | solution.py:437
  41.8 0.0 copy-done
  41.9 0.0 copy-done.1
  41.9 0.0 copy-done.2
  41.9 0.0 copy-done.3
  41.9 0.0 copy-start.4
  41.9 1.0 %copy-done.4 = f32[4,16,1280]{2,1,0:T(8,128)S(1)} copy-done((f32[4,16,1280]{2,1,0:T(8,128)S(1)}, f32[4,16,1280]{2,1,0:T(8,128)}, u32[]{:S(2)}) %copy-start.4) | copy-done | bytes 327704
  42.9 0.0 copy-start.5
  42.9 0.7 %copy-done.5 = f32[8,128]{1,0:T(8,128)S(1)} copy-done((f32[8,128]{1,0:T(8,128)S(1)}, f32[8,128]{1,0:T(8,128)}, u32[]{:S(2)}) %copy-start.5) | copy-done | bytes 4120
  43.5 1.5 %shard_map.95 = (f32[4,16,1280]{2,1,0:T(8,128)}, f32[4,4,16,1280]{3,2,1,0:T(8,128)}, f32[4,16,1280]{2,1,0:T(8,128)}) custom-call(f32[8,128]{1,0:T(8,128)S(1)} %copy-done.5, f32[4,16,1280]{2,1,0:T(8,128)S(1)} %copy-done.4, f32[4,16,1280]{2,1,0:T(8,128)S(1)} %bitcast.15, f32[4,4,16,1280]{3,2,1,0:T(8,128)S(1)} %bitcast.11, f32[4,16,1280]{2,1,0:T(8,128)S(1)} %bitcast.17, ...), custom_call_target="tpu_custom_call" | custom-call | tf_op jit(solution)/shard_map/pallas_call | solution.py:463
Async XLA Ops:
  0.6 41.2 %copy-start = (f32[1,4,4,16,1280]{4,3,2,1,0:T(8,128)S(1)}, f32[1,4,4,16,1280]{4,3,2,1,0:T(8,128)}, u32[]{:S(2)}) copy-start(f32[1,4,4,16,1280]{4,3,2,1,0:T(8,128)} %param.8) | copy-start | bytes 3932164
  0.6 41.2 %copy-start.1 = (f32[1,4,4,16,1280]{4,3,2,1,0:T(8,128)S(1)}, f32[1,4,4,16,1280]{4,3,2,1,0:T(8,128)}, u32[]{:S(2)}) copy-start(f32[1,4,4,16,1280]{4,3,2,1,0:T(8,128)} %param.12) | copy-start | bytes 3932164
  0.7 41.2 %copy-start.2 = (f32[1,4,16,1280]{3,2,1,0:T(8,128)S(1)}, f32[1,4,16,1280]{3,2,1,0:T(8,128)}, u32[]{:S(2)}) copy-start(f32[1,4,16,1280]{3,2,1,0:T(8,128)} %param.7) | copy-start | bytes 983044
  0.7 41.2 %copy-start.3 = (f32[1,4,16,1280]{3,2,1,0:T(8,128)S(1)}, f32[1,4,16,1280]{3,2,1,0:T(8,128)}, u32[]{:S(2)}) copy-start(f32[1,4,16,1280]{3,2,1,0:T(8,128)} %param.11) | copy-start | bytes 983044
  41.9 1.0 %copy-start.4 = (f32[4,16,1280]{2,1,0:T(8,128)S(1)}, f32[4,16,1280]{2,1,0:T(8,128)}, u32[]{:S(2)}) copy-start(f32[4,16,1280]{2,1,0:T(8,128)} %get-tuple-element.9.zdx_h) | copy-start | bytes 983044
  42.9 0.7 %copy-start.5 = (f32[8,128]{1,0:T(8,128)S(1)}, f32[8,128]{1,0:T(8,128)}, u32[]{:S(2)}) copy-start(f32[8,128]{1,0:T(8,128)} %get-tuple-element.8.coef_h) | copy-start | bytes 12292

commit v4 on v3

--- a/solution.py
+++ b/solution.py
@@ -112,7 +112,8 @@
         rim[0, l:l + 1, :] = rs[l, 0:1, :]
         rim[1, l:l + 1, :] = rs[l, last:rows, :]
     tm_send(3, rim, rim_next)
-    tm_send(0, rs, lam_next)
+    for l in range(lev):
+        tm_send(4 + l, rs.at[l], lam_next.at[l])
     loads["mv"].wait()
 
     def _(l):
@@ -197,6 +198,9 @@
     def adjoint1(j):
         if j > 0:
             def _(l):
+                if j == steps - 1:
+                    tm_recv(4 + l, rs.at[l], lam_next.at[l])
+                    t1[l] = mask(j, l) * ro[j, l] - lam_next[l]
                 t1[l] = transposed(t1, j, l) + mask(j - 1, l) * ro[j - 1, l]
         else:
             def _(l):
@@ -282,12 +286,6 @@
             if r == 0:
                 tm_recv(3, rim, rim_next)
             send_adjoint(r, t1, j)
-            if r == 0:
-                tm_recv(0, rs, lam_next)
-
-                def _(l):
-                    t1[l] = mask(steps - 1, l) * ro[steps - 1, l] - lam_next[l]
-                levels(_)
             if j > 0:
                 for name in ("mk", "ro", "wn", "we"):
                     loads[name, j - 1].wait()
@@ -382,7 +380,8 @@
     @pl.when(has_prev)
     def _():
         tm_copy(3, rim, rim_next, tm - 1).wait_send()
-        tm_copy(0, rs, lam_next, tm - 1).wait_send()
+        for l in range(lev):
+            tm_copy(4 + l, rs.at[l], lam_next.at[l], tm - 1).wait_send()
         tm_copy(1, zl, zl_next, tm - 1).wait_send()
         tm_copy(2, u, u_next, tm - 1).wait_send()
     out.wait()
@@ -452,11 +451,11 @@
             pltpu.VMEM((ntm - 1, 8, 128), f32),
             pltpu.VMEM((nsp - 1, 8, 128), f32),
             dma((2 + 5 * steps,)), dma((slots,)), dma((slots,)), dma((slots,)), dma((slots,)),
-            dma((4,)), dma((4,)),
+            dma((4 + lev,)), dma((4 + lev,)),
             dma((ntm - 1,)), dma((ntm - 1,)), dma((nsp - 1,)), dma((nsp - 1,)), dma,
         ],
         compiler_params=pltpu.CompilerParams(
-            collective_id=0, has_side_effects=True, vmem_limit_bytes=56 * 1024 * 1024
+            collective_id=0, has_side_effects=True, vmem_limit_bytes=54656 * 1024
         ),
     )(rhs_state, rhs_obs, wind_east, wind_north, model_var, obs_var, obs_mask)
     vmem = pl.BlockSpec(memory_space=pltpu.VMEM)

time: 45.2 us -> 43.1 us (0.954)
  local copies, waits for them, and re-layouts: 1.66 us -> 0.02 us
    unnamed x12 -> x8, local copies, waits for them, and re-layouts: 1.66 us -> 0.02 us
where the time goes in v4:
time: 43.1 us; the launch traced here: 43 us
  Pallas kernels  42.3 us (98%)
  between operations  0.7 us (2%)
    pallas_call x1, Pallas kernels, on_device(): pl.pallas_call(functools.partial(kernel, ntm, nsp), out_shape=(jax.ShapeD...  40.7 us
    pallas_call x1, Pallas kernels, on_device(): pl.pallas_call(combine, out_shape=(jax.ShapeDtypeStruct((lev, rows, nlon)...  1.53 us

profile of v4, /device:TPU:0, one launch (start us, length us, event | category | flops | bytes accessed | tf_op | source)
XLA Modules:
  0.0 43.0 jit_solution(12416886524830254825)
XLA Ops:
  0.6 0.0 copy-start
  0.6 0.0 copy-start.1
  0.7 0.0 copy-start.2
  0.7 0.0 copy-start.3
  0.7 40.7 %shard_map.94 = (f32[4,16,1280]{2,1,0:T(8,128)S(1)}, f32[8,128]{1,0:T(8,128)S(1)}) custom-call(f32[4,16,1280]{2,1,0:T(8,128)} %bitcast.14, f32[4,4,16,1280]{3,2,1,0:T(8,128)} %bitcast.10, f32[4,4,16,1280]{3,2,1,0:T(8,128)} %bitcast.18, f32[4,4,16,1280]{3,2,1,0:T(8,128)} %bitcast.19, f32[4,16,1280]{2,1,0:T(8,128)} %bitcast.16, f32[4,4,16,1280]{3,2,1,0:T(8,128)} %bitcast.12, ...), custom_call_target="tpu_custom_call" | custom-call | tf_op jit(solution)/shard_map/pallas_call | solution.py:436
  41.4 0.0 copy-done
  41.4 0.0 copy-done.1
  41.4 0.0 copy-done.2
  41.4 0.0 copy-done.3
  41.5 1.5 %shard_map.95 = (f32[4,16,1280]{2,1,0:T(8,128)}, f32[4,4,16,1280]{3,2,1,0:T(8,128)}, f32[4,16,1280]{2,1,0:T(8,128)}) custom-call(f32[8,128]{1,0:T(8,128)S(1)} %get-tuple-element.8.coef_h, f32[4,16,1280]{2,1,0:T(8,128)S(1)} %get-tuple-element.9.zdx_h, f32[4,16,1280]{2,1,0:T(8,128)S(1)} %bitcast.15, f32[4,4,16,1280]{3,2,1,0:T(8,128)S(1)} %bitcast.11, ...), custom_call_target="tpu_custom_call" | custom-call | tf_op jit(solution)/shard_map/pallas_call | solution.py:462
Async XLA Ops:
  0.6 40.8 %copy-start = (f32[1,4,4,16,1280]{4,3,2,1,0:T(8,128)S(1)}, f32[1,4,4,16,1280]{4,3,2,1,0:T(8,128)}, u32[]{:S(2)}) copy-start(f32[1,4,4,16,1280]{4,3,2,1,0:T(8,128)} %param.8) | copy-start | bytes 3932164
  0.6 40.8 %copy-start.1 = (f32[1,4,4,16,1280]{4,3,2,1,0:T(8,128)S(1)}, f32[1,4,4,16,1280]{4,3,2,1,0:T(8,128)}, u32[]{:S(2)}) copy-start(f32[1,4,4,16,1280]{4,3,2,1,0:T(8,128)} %param.12) | copy-start | bytes 3932164
  0.7 40.8 %copy-start.2 = (f32[1,4,16,1280]{3,2,1,0:T(8,128)S(1)}, f32[1,4,16,1280]{3,2,1,0:T(8,128)}, u32[]{:S(2)}) copy-start(f32[1,4,16,1280]{3,2,1,0:T(8,128)} %param.7) | copy-start | bytes 983044
  0.7 40.8 %copy-start.3 = (f32[1,4,16,1280]{3,2,1,0:T(8,128)S(1)}, f32[1,4,16,1280]{3,2,1,0:T(8,128)}, u32[]{:S(2)}) copy-start(f32[1,4,16,1280]{3,2,1,0:T(8,128)} %param.11) | copy-start | bytes 983044

commit v5 on v4

--- a/solution.py
+++ b/solution.py
@@ -48,11 +48,21 @@
         load(("ov", j), ov_h.at[j], ov.at[j])
 
     barrier = pltpu.get_barrier_semaphore()
-    for d in range(1, ntm):
-        pl.semaphore_signal(barrier, inc=1, device_id=(lax.rem(tm + d, ntm), sp), device_id_type=MESH)
-    for d in range(1, nsp):
-        pl.semaphore_signal(barrier, inc=1, device_id=(tm, lax.rem(sp + d, nsp)), device_id_type=MESH)
-    pl.semaphore_wait(barrier, ntm + nsp - 2)
+    total_devices = ntm * nsp
+    flat = total_devices <= 64
+
+    def any_device(d):
+        at = lax.rem(tm * nsp + sp + d, total_devices)
+        return (lax.div(at, nsp), lax.rem(at, nsp))
+
+    if flat:
+        peers = [any_device(d) for d in range(1, total_devices)]
+    else:
+        peers = [(lax.rem(tm + d, ntm), sp) for d in range(1, ntm)]
+        peers += [(tm, lax.rem(sp + d, nsp)) for d in range(1, nsp)]
+    for peer in peers:
+        pl.semaphore_signal(barrier, inc=1, device_id=peer, device_id_type=MESH)
+    pl.semaphore_wait(barrier, len(peers))
 
     def tm_copy(i, src, dst, device):
         return pltpu.make_async_remote_copy(
@@ -351,13 +361,17 @@
             total = total + slots[d]
         return total, copies
 
-    total, copies1 = gather(
-        ntm, part_tm, ptm_s, ptm_r, lambda d: (lax.rem(tm + d, ntm), sp), part.at[0]
-    )
-    part[1] = total
-    total, copies2 = gather(
-        nsp, part_sp, psp_s, psp_r, lambda d: (tm, lax.rem(sp + d, nsp)), part.at[1]
-    )
+    copies1 = []
+    if flat:
+        total, copies2 = gather(total_devices, part_sp, psp_s, psp_r, any_device, part.at[0])
+    else:
+        total, copies1 = gather(
+            ntm, part_tm, ptm_s, ptm_r, lambda d: (lax.rem(tm + d, ntm), sp), part.at[0]
+        )
+        part[1] = total
+        total, copies2 = gather(
+            nsp, part_sp, psp_s, psp_r, lambda d: (tm, lax.rem(sp + d, nsp)), part.at[1]
+        )
     sums = jnp.broadcast_to(jnp.sum(total, axis=1, keepdims=True), (8, 128))
     n, d, e, f = (sums[i:i + 1, :] for i in range(4))
     first = n / d
@@ -429,6 +443,7 @@
     field = pltpu.VMEM((lev, rows, nlon), f32)
     fields = pltpu.VMEM((steps, lev, rows, nlon), f32)
     slots = 3 * steps
+    far = ntm * nsp - 1 if ntm * nsp <= 64 else nsp - 1
     halo = pltpu.VMEM((slots, lev, nlon), f32)
     rim = pltpu.VMEM((2, lev, nlon), f32)
     dma = pltpu.SemaphoreType.DMA
@@ -449,10 +464,10 @@
             pltpu.VMEM((4, lev, 8, nlon), f32), halo, halo, halo, halo,
             pltpu.VMEM((2, 8, 128), f32),
             pltpu.VMEM((ntm - 1, 8, 128), f32),
-            pltpu.VMEM((nsp - 1, 8, 128), f32),
+            pltpu.VMEM((far, 8, 128), f32),
             dma((2 + 5 * steps,)), dma((slots,)), dma((slots,)), dma((slots,)), dma((slots,)),
             dma((4 + lev,)), dma((4 + lev,)),
-            dma((ntm - 1,)), dma((ntm - 1,)), dma((nsp - 1,)), dma((nsp - 1,)), dma,
+            dma((ntm - 1,)), dma((ntm - 1,)), dma((far,)), dma((far,)), dma,
         ],
         compiler_params=pltpu.CompilerParams(
             collective_id=0, has_side_effects=True, vmem_limit_bytes=54656 * 1024

time: 43.1 us -> 43.7 us (1.014)
  Pallas kernels: 42.3 us -> 42.8 us
    pallas_call x1, Pallas kernels: 40.7 us -> 41.3 us  [on_device(): pl.pallas_call(functools.partial(kernel, ntm, nsp), out_shape=(jax.ShapeD...]
where the time goes in v5:
time: 43.7 us; the launch traced here: 43.6 us
  Pallas kernels  42.8 us (98%)
  between operations  0.7 us (2%)
    pallas_call x1, Pallas kernels, on_device(): pl.pallas_call(functools.partial(kernel, ntm, nsp), out_shape=(jax.ShapeD...  41.3 us
    pallas_call x1, Pallas kernels, on_device(): pl.pallas_call(combine, out_shape=(jax.ShapeDtypeStruct((lev, rows, nlon)...  1.53 us

profile of v5, /device:TPU:0, one launch (start us, length us, event | category | flops | bytes accessed | tf_op | source)
XLA Modules:
  0.0 43.6 jit_solution(9389468808935190375)
XLA Ops:
  0.6 0.0 copy-start
  0.6 0.0 copy-start.1
  0.7 0.0 copy-start.2
  0.7 0.0 copy-start.3
  0.7 41.3 %shard_map.94 = (f32[4,16,1280]{2,1,0:T(8,128)S(1)}, f32[8,128]{1,0:T(8,128)S(1)}) custom-call(f32[4,16,1280]{2,1,0:T(8,128)} %bitcast.14, f32[4,4,16,1280]{3,2,1,0:T(8,128)} %bitcast.10, f32[4,4,16,1280]{3,2,1,0:T(8,128)} %bitcast.18, f32[4,4,16,1280]{3,2,1,0:T(8,128)} %bitcast.19, f32[4,16,1280]{2,1,0:T(8,128)} %bitcast.16, f32[4,4,16,1280]{3,2,1,0:T(8,128)} %bitcast.12, ...), custom_call_target="tpu_custom_call" | custom-call | tf_op jit(solution)/shard_map/pallas_call | solution.py:451
  42.0 0.0 copy-done
  42.0 0.0 copy-done.1
  42.0 0.0 copy-done.2
  42.0 0.0 copy-done.3
  42.0 1.5 %shard_map.95 = (f32[4,16,1280]{2,1,0:T(8,128)}, f32[4,4,16,1280]{3,2,1,0:T(8,128)}, f32[4,16,1280]{2,1,0:T(8,128)}) custom-call(f32[8,128]{1,0:T(8,128)S(1)} %get-tuple-element.8.coef_h, f32[4,16,1280]{2,1,0:T(8,128)S(1)} %get-tuple-element.9.zdx_h, f32[4,16,1280]{2,1,0:T(8,128)S(1)} %bitcast.15, f32[4,4,16,1280]{3,2,1,0:T(8,128)S(1)} %bitcast.11, ...), custom_call_target="tpu_custom_call" | custom-call | tf_op jit(solution)/shard_map/pallas_call | solution.py:477
Async XLA Ops:
  0.6 41.4 %copy-start = (f32[1,4,4,16,1280]{4,3,2,1,0:T(8,128)S(1)}, f32[1,4,4,16,1280]{4,3,2,1,0:T(8,128)}, u32[]{:S(2)}) copy-start(f32[1,4,4,16,1280]{4,3,2,1,0:T(8,128)} %param.8) | copy-start | bytes 3932164
  0.6 41.4 %copy-start.1 = (f32[1,4,4,16,1280]{4,3,2,1,0:T(8,128)S(1)}, f32[1,4,4,16,1280]{4,3,2,1,0:T(8,128)}, u32[]{:S(2)}) copy-start(f32[1,4,4,16,1280]{4,3,2,1,0:T(8,128)} %param.12) | copy-start | bytes 3932164
  0.7 41.4 %copy-start.2 = (f32[1,4,16,1280]{3,2,1,0:T(8,128)S(1)}, f32[1,4,16,1280]{3,2,1,0:T(8,128)}, u32[]{:S(2)}) copy-start(f32[1,4,16,1280]{3,2,1,0:T(8,128)} %param.7) | copy-start | bytes 983044
  0.7 41.4 %copy-start.3 = (f32[1,4,16,1280]{3,2,1,0:T(8,128)S(1)}, f32[1,4,16,1280]{3,2,1,0:T(8,128)}, u32[]{:S(2)}) copy-start(f32[1,4,16,1280]{3,2,1,0:T(8,128)} %param.11) | copy-start | bytes 983044
